TPU v7x, 32 devices: a whole 2x2x4 slice. The times are simulated.
32 devices in a mesh: rows: 8 (over z, y), grp: 4 (over x, core).
Axes of the slice: x: 2, y: 2, z: 4, core: 2. Of those that a mesh axis runs over, the one named last changes fastest.
Arguments:
- features: bfloat16 [192, 128, 2048], P('rows', None, 'grp'), may hold values from 0 to 12
- depth_weight: float32 [3, 3, 3, 2048], P(None, None, None, 'grp'), may hold values from -2 to 2
- branch_weight: bfloat16 [4, 2048, 256], P(None, 'grp'), may hold values from -0.125 to 0.125
- pool_weight: bfloat16 [2048, 256], P('grp'), may hold values from -0.125 to 0.125
- proj_weight: bfloat16 [5, 256, 256], P(None, 'grp'), may hold values from -0.15625 to 0.15625
- class_weight: bfloat16 [256, 11], replicated, may hold values from -0.375 to 0.375
- labels: int32 [192, 128], P('rows'), may hold values from 0 to 11
Outputs:
- grad_branch: float32 [4, 2048, 256], P(None, 'grp')
- grad_depth: float32 [3, 3, 3, 2048], P(None, None, None, 'grp')
- grad_pool: float32 [2048, 256], P('grp')
- grad_proj: float32 [5, 256, 256], P(None, 'grp')
- grad_class: float32 [256, 11], replicated
All inputs are finite; a program needn't handle non-finite values.
Results may differ from a plain program's by a relative error of at most 0.0056.
Values may be sent and summed in bfloat16 or wider, within the bound.
A program may use at most 128 MiB of HBM per device.

v0:
```python
import math

import jax
import jax.numpy as jnp
from jax import lax
from jax.sharding import PartitionSpec as P

RATES = (6, 12, 18)
MARGIN = 18


def padded_2(block, sides, width):
    for axis, dim in sides:
        count = lax.axis_size(axis)
        forward = [(i, i + 1) for i in range(count - 1)]
        backward = [(target, source) for source, target in forward]
        low = lax.ppermute(
            lax.slice_in_dim(block, block.shape[dim] - width, None, axis=dim), axis, forward
        )
        high = lax.ppermute(lax.slice_in_dim(block, 0, width, axis=dim), axis, backward)
        block = jnp.concatenate([low, block, high], axis=dim)
    return block


def depth_taps(padded, weights, height, width):
    outputs = []
    for index, rate in enumerate(RATES):
        total = jnp.zeros((height, width, padded.shape[2]), jnp.float32)
        for row_tap in range(3):
            for col_tap in range(3):
                row_start = MARGIN + (row_tap - 1) * rate
                col_start = MARGIN + (col_tap - 1) * rate
                total = (
                    total
                    + weights[index, row_tap, col_tap]
                    * padded[row_start : row_start + height, col_start : col_start + width]
                )
        outputs.append(total.astype(jnp.bfloat16))
    return outputs


def depth_grads(padded, backs, height, width):
    result = []
    for index, rate in enumerate(RATES):
        taps = []
        for row_tap in range(3):
            for col_tap in range(3):
                row_start = MARGIN + (row_tap - 1) * rate
                col_start = MARGIN + (col_tap - 1) * rate
                window = padded[row_start : row_start + height, col_start : col_start + width]
                taps.append(jnp.sum(backs[index] * window, axis=(0, 1)))
        result.append(jnp.stack(taps).reshape(3, 3, -1))
    return jnp.stack(result)


def class_head(mixed, class_weight, labels, total_pixels):
    f32 = jnp.float32
    classes = class_weight.shape[1]
    hidden = jnp.maximum(mixed, 0.0).astype(jnp.bfloat16)
    logits = jnp.einsum("pc,ck->kp", hidden, class_weight, preferred_element_type=f32)
    expo = jnp.exp(logits)
    soft = expo / jnp.sum(expo, axis=0, keepdims=True)
    label_row = labels.reshape(-1)
    onehot = (
        lax.broadcasted_iota(jnp.int32, (classes, label_row.shape[0]), 0) == label_row[None, :]
    ).astype(f32)
    valid = (label_row < classes).astype(f32)
    grad_logit = ((soft - onehot) * valid[None, :] / math.sqrt(total_pixels)).astype(jnp.bfloat16)
    class_part = jnp.einsum("pc,kp->ck", hidden, grad_logit, preferred_element_type=f32)
    back_hidden = jnp.einsum("ck,kp->pc", class_weight, grad_logit, preferred_element_type=f32)
    grad_mixed = (back_hidden * (mixed > 0)).astype(jnp.bfloat16)
    col_total = lax.psum(jnp.sum(grad_mixed.astype(f32), axis=0), "rows")
    return (grad_mixed, col_total, class_part)


def per_device(
    features, depth_weight, branch_weight, pool_weight, proj_weight, class_weight, labels
):
    f32 = jnp.float32
    highest = lax.Precision.HIGHEST
    height, width, local_in = features.shape
    pixels_local = height * width
    total_pixels = height * lax.axis_size("rows") * width
    halo_rows = padded_2(features, (("rows", 0),), MARGIN)
    padded = jnp.pad(halo_rows.astype(f32), ((0, 0), (MARGIN, MARGIN), (0, 0)))
    depth_out = depth_taps(padded, depth_weight, height, width)
    flat_inputs = [item.reshape(pixels_local, local_in) for item in [features] + depth_out]
    column_sum = jnp.sum(features.astype(f32), axis=(0, 1))
    pooled = lax.psum(column_sum, "rows") / total_pixels
    partial_pre = jnp.stack(
        [jnp.dot(flat_inputs[k], branch_weight[k], preferred_element_type=f32) for k in range(4)]
    )
    pool_part = jnp.dot(pooled, pool_weight.astype(f32), precision=highest)[None, None, :]
    pre, pool_pre = (
        lax.psum_scatter(partial_pre, "grp", scatter_dimension=2, tiled=True),
        lax.psum_scatter(pool_part, "grp", scatter_dimension=2, tiled=True),
    )
    pool_pre = pool_pre[0, 0]
    own_out = jnp.maximum(pre, 0.0).astype(jnp.bfloat16)
    own_pool = jnp.maximum(pool_pre, 0.0).astype(jnp.bfloat16)
    mixed_part = jnp.einsum("kpc,kcd->pd", own_out, proj_weight[:4], preferred_element_type=f32)
    mixed_part = (
        mixed_part
        + jnp.dot(own_pool.astype(f32), proj_weight[4].astype(f32), precision=highest)[None, :]
    )
    mixed = lax.psum(mixed_part, "grp")
    grad_mixed, col_total, class_part = class_head(mixed, class_weight, labels, total_pixels)
    back_pre = jnp.einsum("pd,kcd->kpc", grad_mixed, proj_weight[:4], preferred_element_type=f32)
    own_grad = (back_pre * (pre > 0)).astype(jnp.bfloat16)
    own_poolgrad = (
        jnp.dot(col_total, proj_weight[4].astype(f32).T, precision=highest) * (pool_pre > 0)
    ).astype(jnp.bfloat16)
    grad_pre, grad_poolpre = (
        lax.all_gather(own_grad, "grp", axis=2, tiled=True),
        lax.all_gather(own_poolgrad[None, None, :], "grp", axis=2, tiled=True),
    )
    grad_poolpre = grad_poolpre[0, 0]
    proj_part = jnp.einsum("kpc,pd->kcd", own_out, grad_mixed, preferred_element_type=f32)
    pool_proj = own_pool.astype(f32)[:, None] * col_total[None, :]
    branch_part = jnp.stack(
        [
            jnp.einsum("pc,pd->cd", flat_inputs[k], grad_pre[k], preferred_element_type=f32)
            for k in range(4)
        ]
    )
    backs = [
        jnp.einsum(
            "pd,cd->pc", grad_pre[k + 1], branch_weight[k + 1], preferred_element_type=f32
        ).reshape(height, width, local_in)
        for k in range(3)
    ]
    depth_part = depth_grads(padded, backs, height, width)
    grad_pool = pooled[:, None] * grad_poolpre.astype(f32)[None, :]
    grad_branch, grad_depth, proj_main, grad_class = lax.psum(
        (branch_part, depth_part, proj_part, class_part), "rows"
    )
    grad_proj = jnp.concatenate([proj_main, pool_proj[None]], axis=0)
    return (grad_branch, grad_depth, grad_pool, grad_proj, grad_class)


def solution(mesh):
    return jax.shard_map(
        per_device,
        mesh=mesh,
        in_specs=(
            P("rows", None, "grp"),
            P(None, None, None, "grp"),
            P(None, "grp", None),
            P("grp", None),
            P(None, "grp", None),
            P(),
            P("rows", None),
        ),
        out_specs=(
            P(None, "grp", None),
            P(None, None, None, "grp"),
            P("grp", None),
            P(None, "grp", None),
            P(),
        ),
        check_vma=False,
    )
```

profile of v0, /device:TPU:29, one launch (start us, length us, event | category | flops | bytes accessed | tf_op | source)
XLA Modules:
  0.0 924.8 jit_solution(12588569372178841400)
XLA Ops:
  7.2 5.2 fusion.69
  12.4 1.3 collective-permute-start
  13.7 5.4 collective-permute-start.1
  19.6 105.5 %psum.49 = f32[512]{0:T(512)S(1)} all-reduce(f32[512]{0:T(512)S(1)} %convert_reduce_fusion), channel_id=1, replica_groups=mesh['rows'=8,'grp'=4] {'rows'}, use_global_device_ids=true, to_apply=%region_2.3 | all-reduce | flops 512 | bytes 4096 | tf_op jit(solution)/shard_map/psum | solution.py:89
  126.3 1.9 convolution_bitcast_fusion.5
  128.2 8.3 maximum_convert_fusion
  136.5 24.1 %add_convert_fusion.1 = bf16[24,128,512]{2,1,0:T(8,128)(2,1)S(1)} fusion(f32[60,128,512]{2,1,0:T(8,128)} %maximum_convert_fusion, f32[512]{0:T(512)S(1)} %bitcast.242, f32[512]{0:T(512)S(1)} %bitcast.243, f32[512]{0:T(512)S(1)} %bitcast.244, f32[512]{0:T(512)S(1)} %bitcast.245, f32[512]{0:T(512)S(1)} %bitcast.246, f32[512]{0:T(512)S(1)} %bitcast.247, ...), kind=kLoop, calls=%fused_computation.49 | loop fusion | flops 28311552 | bytes 37767168 | tf_op jit(solution)/shard_map/convert_element_type | solution.py:38
  160.6 2.1 convolution_bitcast_fusion.3
  162.7 19.2 %add_convert_fusion = bf16[24,128,512]{2,1,0:T(8,128)(2,1)S(1)} fusion(f32[60,128,512]{2,1,0:T(8,128)} %maximum_convert_fusion, f32[512]{0:T(512)S(1)} %bitcast.230, f32[512]{0:T(512)S(1)} %bitcast.231, f32[512]{0:T(512)S(1)} %bitcast.235, f32[512]{0:T(512)S(1)} %bitcast.236, f32[512]{0:T(512)S(1)} %bitcast.237, f32[512]{0:T(512)S(1)} %bitcast.238, ...), kind=kLoop, calls=%fused_computation.48 | loop fusion | flops 28311552 | bytes 37767168 | tf_op jit(solution)/shard_map/convert_element_type | solution.py:38
  182.0 1.7 copy-done.3
  183.7 3.6 convolution_bitcast_fusion.2
  187.3 24.6 %add_convert_fusion.2 = bf16[24,128,512]{2,1,0:T(8,128)(2,1)S(1)} fusion(f32[60,128,512]{2,1,0:T(8,128)} %maximum_convert_fusion, f32[512]{0:T(512)S(1)} %bitcast.233, f32[512]{0:T(512)S(1)} %bitcast.234, f32[512]{0:T(512)S(1)} %bitcast.225, f32[512]{0:T(512)S(1)} %bitcast.226, f32[512]{0:T(512)S(1)} %bitcast.227, f32[512]{0:T(512)S(1)} %bitcast.228, ...), kind=kLoop, calls=%fused_computation.50 | loop fusion | flops 28311552 | bytes 37767168 | tf_op jit(solution)/shard_map/convert_element_type | solution.py:38
  211.9 1.6 copy-done.5
  213.5 2.4 convolution_bitcast_fusion.4
  215.9 4.9 pad_maximum_fusion
  220.8 15.3 %copy.30 = f32[4,3072,256]{1,0,2:T(4,128)} copy(f32[4,3072,256]{2,1,0:T(8,128)} %pad_maximum_fusion) | data formatting | bytes 25165824 | tf_op jit(solution)/shard_map/stack | solution.py:90
  239.0 221.1 %all-reduce.12.cloned.1.call-done = f32[4,3072,256]{1,0,2:T(4,128)} async-done(((f32[4,3072,256]{1,0,2:T(4,128)}), f32[4,3072,256]{1,0,2:T(4,128)}) %all-reduce.12.cloned.1.call-update) | async-done | bytes 12582928
  460.1 2.1 constant_dynamic-slice_fusion
  462.2 1.6 copy-done.7
  463.8 3.8 fusion.1
  467.7 68.9 %all-reduce.10.cloned.1.call-done = f32[3072,256]{1,0:T(8,128)} async-done(((f32[3072,256]{1,0:T(8,128)}), f32[3072,256]{1,0:T(8,128)}) %all-reduce.10.cloned.1.call-update) | async-done | bytes 3145744 | tf_op jit(solution)/shard_map/psum | solution.py:106
  536.6 2.6 fusion.73
  539.2 3.2 convert_reduce_fusion.1
  542.4 3.3 fusion.3
  545.8 2.4 copy.33
  548.2 2.8 fusion.29
  551.0 5.0 fusion.12
  556.0 39.3 %all-gather.3.cloned.1.call-done = bf16[4,3072,256]{1,0,2:T(4,128)(2,1)} async-done(((bf16[4,3072,64]{1,0,2:T(4,128)(2,1)}), bf16[4,3072,256]{1,0,2:T(4,128)(2,1)}) %all-gather.3.cloned.1.call-update) | async-done | bytes 6291472 | tf_op jit(solution)/shard_map/all_gather | solution.py:114
  595.3 18.8 %fusion.68 = (bf16[1,3072,256]{1,0,2:T(2,128)(2,1)}, bf16[1,3072,256]{1,0,2:T(2,128)(2,1)}, bf16[1,3072,256]{1,0,2:T(2,128)(2,1)}, bf16[1,3072,256]{1,0,2:T(2,128)(2,1)}) fusion(bf16[4,3072,256]{1,0,2:T(4,128)(2,1)} %all-gather.3.cloned.1.call-done), kind=kLoop, calls=%fused_computation.133 | loop fusion | bytes 12582912 | tf_op jit(solution)/shard_map/slice | solution.py:122
  614.1 7.3 copy.48
  621.4 4.3 fusion.18
  625.7 24.8 %multiply_reduce_fusion.18 = (f32[512]{0:T(512)S(1)}, f32[512]{0:T(512)S(1)}, f32[512]{0:T(512)S(1)}, f32[512]{0:T(512)S(1)}, f32[512]{0:T(512)S(1)}, /*index=5*...) fusion(f32[60,128,512]{2,1,0:T(8,128)} %maximum_convert_fusion, ...), kind=kOutput, calls=%fused_computation.38 | convolution fusion | flops 833613312 | bytes 36456448 | tf_op jit(solution)/shard_map/pd,cd->pc/dot_general | solution.py:127
  650.5 7.3 copy.49
  657.9 4.3 fusion.21
  662.2 24.1 %multiply_reduce_fusion.9 = (f32[512]{0:T(512)S(1)}, f32[512]{0:T(512)S(1)}, f32[512]{0:T(512)S(1)}, f32[512]{0:T(512)S(1)}, f32[512]{0:T(512)S(1)}, /*index=5*/...) fusion(f32[60,128,512]{2,1,0:T(8,128)} %maximum_convert_fusion, ...), kind=kOutput, calls=%fused_computation.29 | convolution fusion | flops 833613312 | bytes 36456448 | tf_op jit(solution)/shard_map/pd,cd->pc/dot_general | solution.py:127
  686.3 7.3 copy.50
  693.6 4.2 fusion.24
  697.8 20.2 %multiply_reduce_fusion = (f32[512]{0:T(512)S(1)}, f32[512]{0:T(512)S(1)}, f32[512]{0:T(512)S(1)}, f32[512]{0:T(512)S(1)}, f32[512]{0:T(512)S(1)}, /*index=5*/f3...) fusion(f32[60,128,512]{2,1,0:T(8,128)} %maximum_convert_fusion, bf16[24,128,256]{2,1,0:T(8,128)(2,1)} %bitcast.217, ...), kind=kOutput, calls=%fused_computation.20 | convolution fusion | flops 833613312 | bytes 36456448 | tf_op jit(solution)/shard_map/pd,cd->pc/dot_general | solution.py:127
  718.1 7.3 copy.47
  725.5 3.2 fusion.15
  729.4 3.0 pad_maximum_fusion.1
  733.1 62.9 %all-reduce.14.cloned.1.call-done = (f32[3,3,3,512]{3,2,1,0:T(4,128)}, f32[256]{0:T(256)}, f32[256,11]{0,1:T(8,128)}) async-done(((f32[3,3,3,512]{3,2,1,0:T(4,128)}, f32[256]{0:T(256)}, f32[256,11]{0,1:T(8,128)}), (f32[3,3,3,512]{3,2,1,0:T(4,128)}, f32[256]{0:T(256)}, f32[256,11]{0,1:T(8,128)})) %all-reduce.14.cloned.1.call-update) | async-done | bytes 67600 | tf_op jit(solution)/shard_map/psum | solution.py:134
  797.1 7.2 all-reduce.1
  806.0 104.3 %all-reduce.16.cloned.1.call-done = (f32[4,512,256]{1,2,0:T(8,128)}, f32[4,64,256]{2,1,0:T(8,128)}) async-done(((f32[4,512,256]{1,2,0:T(8,128)}, f32[4,64,256]{2,1,0:T(8,128)}), (f32[4,512,256]{1,2,0:T(8,128)}, f32[4,64,256]{2,1,0:T(8,128)})) %all-reduce.16.cloned.1.call-update) | async-done | bytes 2359312 | tf_op jit(solution)/shard_map/psum | solution.py:134
  910.2 2.9 copy.41
  913.1 1.7 pad_maximum_fusion.2
  914.8 1.5 copy.63
  916.3 1.3 copy.64
  (69 shorter events, 7.9 us)
Async XLA Ops:
  7.2 117.9 %copy-start = (bf16[512,256]{1,0:T(8,128)(2,1)S(1)}, bf16[512,256]{1,0:T(8,128)(2,1)}, u32[]{:S(2)}) copy-start(bf16[512,256]{1,0:T(8,128)(2,1)} %param.10) | copy-start | bytes 786436
  7.2 11.9 %copy-start.2 = (bf16[24,128,512]{2,1,0:T(8,128)(2,1)S(1)}, bf16[24,128,512]{2,1,0:T(8,128)(2,1)}, u32[]{:S(2)}) copy-start(bf16[24,128,512]{2,1,0:T(8,128)(2,1)} %param.7) | copy-start | bytes 9437188
  7.2 119.0 %copy-start.13 = (f32[3,3,3,512]{3,2,1,0:T(4,128)S(1)}, f32[3,3,3,512]{3,2,1,0:T(4,128)}, u32[]{:S(2)}) copy-start(f32[3,3,3,512]{3,2,1,0:T(4,128)} %param.8) | copy-start | bytes 165892
  7.2 230.9 %reduce-scatter.4.cloned.1.call-start = ((), (), s32[]{:S(2)}) async-start(), calls=%async_computation.3 | async-start | bytes 163840
  12.4 115.8 %collective-permute-start = (bf16[18,128,512]{2,1,0:T(8,128)(2,1)}, bf16[18,128,512]{2,1,0:T(8,128)(2,1)}, u32[]{:S(2)}, u32[]{:S(2)}) collective-permute-start(bf16[18,128,512]{2,1,0:T(8,128)(2,1)} %get-tuple-element.56), channel_id=1, source_target_pairs={{0,4},{4,8},{8,12},{12,16},{16,20},{20,24},{24,28},{1,5},{5,9},{9,... | collective-permute-start | bytes 7077896 | tf_op jit(solution)/shard_map/ppermute | solution.py:17
  13.7 114.5 %collective-permute-start.1 = (bf16[18,128,512]{2,1,0:T(8,128)(2,1)}, bf16[18,128,512]{2,1,0:T(8,128)(2,1)}, u32[]{:S(2)}, u32[]{:S(2)}) collective-permute-start(bf16[18,128,512]{2,1,0:T(8,128)(2,1)} %get-tuple-element.57), channel_id=1, source_target_pairs={{4,0},{8,4},{12,8},{16,12},{20,16},{24,20},{28,24},{5,1},{9,5},{13... | collective-permute-start | bytes 7077896 | tf_op jit(solution)/shard_map/ppermute | solution.py:20
  126.1 333.9 %all-reduce.12.cloned.1.call-start = ((), (), s32[]{:S(2)}) async-start(), calls=%async_computation.4 | async-start | bytes 25165824
  160.6 2.1 copy-start.4
  182.0 1.7 copy-start.3
  211.8 1.6 copy-start.5
  211.8 4.0 copy-start.6
  236.1 0.7 copy-start.16
  236.1 2.8 copy-start.15
  236.1 300.5 %all-reduce.10.cloned.1.call-start = ((), (), s32[]{:S(2)}) async-start(), calls=%async_computation.1 | async-start | bytes 6291456 | tf_op jit(solution)/shard_map/psum | solution.py:106
  462.2 1.7 copy-start.7
  462.2 5.5 copy-start.12
  462.2 74.4 %copy-start.14 = (bf16[256,11]{0,1:T(8,128)(2,1)S(1)}, bf16[256,11]{0,1:T(8,128)(2,1)}, u32[]{:S(2)}) copy-start(bf16[256,11]{0,1:T(8,128)(2,1)} %param.12) | copy-start | bytes 16900
  467.7 127.6 %all-gather.3.cloned.1.call-start = ((), (), s32[]{:S(2)}) async-start(), calls=%async_computation.2 | async-start | bytes 7864320 | tf_op jit(solution)/shard_map/all_gather | solution.py:114
  536.6 5.8 copy-start.8
  542.4 3.3 copy-start.9
  548.1 247.8 %all-reduce.14.cloned.1.call-start = ((), (), s32[]{:S(2)}) async-start(), calls=%async_computation.5 | async-start | bytes 182272 | tf_op jit(solution)/shard_map/psum | solution.py:134
  621.4 4.3 copy-start.10
  657.9 4.3 copy-start.11
  725.5 192.2 %copy-start.1 = (bf16[512,256]{1,0:T(8,128)(2,1)S(1)}, bf16[512,256]{1,0:T(8,128)(2,1)}, u32[]{:S(2)}) copy-start(bf16[512,256]{1,0:T(8,128)(2,1)} %param.10) | copy-start | bytes 786436
  729.4 180.9 %all-reduce.16.cloned.1.call-start = ((), (), s32[]{:S(2)}) async-start(), calls=%async_computation.6 | async-start | bytes 4718592 | tf_op jit(solution)/shard_map/psum | solution.py:134
Sparse Core Ops, SparseCore 0:
  126.3 22.4 reduce-scatter.3
  236.2 223.8 all-reduce.11
  467.8 68.7 all-reduce.9
  548.3 47.0 all-gather.2
  729.5 66.4 all-reduce.13
  800.4 109.7 all-reduce.15
where the time goes:
time: 933 us; the launch traced here: 925 us
  waiting for transfers between devices  496 us (53%)
  matrix products  118 us (13%)
  blocking collectives  113 us (12%)
  other arithmetic  88.6 us (9%)
  local copies, waits for them, and re-layouts  86.1 us (9%)
  between operations  16 us (2%)
    unnamed x8, waiting for transfers between devices  221 us
    psum x2, waiting for transfers between devices, per_device(): lax.psum((branch_part, depth_part, proj_part, class_part), 'rows')  167 us
    psum x1, blocking collectives, per_device(): pooled = lax.psum(column_sum, 'rows') / total_pixels  105 us
    dot_general x3, matrix products, per_device(): jnp.einsum('pd,cd->pc', grad_pre[k + 1], branch_weight[k + 1], preferred_...  69.1 us
    psum x1, waiting for transfers between devices, per_device(): mixed = lax.psum(mixed_part, 'grp')  68.9 us
    convert_element_type x3, other arithmetic, depth_taps(): outputs.append(total.astype(jnp.bfloat16))  67.9 us
    unnamed x46, local copies, waits for them, and re-layouts  44.2 us
    all_gather x1, waiting for transfers between devices, per_device(): lax.all_gather(own_grad, 'grp', axis=2, tiled=True)  39.3 us
  transfers between devices with their start and end apart: 8, of which 5 were waited for; matrix products, arithmetic and copies ran while one was open for 13% of the time, Pallas kernels for 0%

commit v1 on v0

v1 whole, which is shorter than its diff:
```python
import functools
import math

import jax
import jax.numpy as jnp
from jax import lax
from jax.experimental import pallas as pl
from jax.experimental.pallas import tpu as pltpu
from jax.sharding import PartitionSpec as P

RATES = (6, 12, 18)
MARGIN = 18
MESH = pl.DeviceIdType.MESH
F32 = jnp.float32
BF16 = jnp.bfloat16
VMEM_LIMIT = 56 * 1024 * 1024


def vspec():
    return pl.BlockSpec(memory_space=pltpu.VMEM)


def remote(src, dst, send, recv, rows_at, grp_at):
    return pltpu.make_async_remote_copy(
        src_ref=src,
        dst_ref=dst,
        send_sem=send,
        recv_sem=recv,
        device_id=(rows_at, grp_at),
        device_id_type=MESH,
    )


def greet(places):
    barrier = pltpu.get_barrier_semaphore()
    for place in places:
        pl.semaphore_signal(barrier, inc=1, device_id=place, device_id_type=MESH)
    pl.semaphore_wait(barrier, len(places))


def places_of(n_rows, n_grp, me_r, me_g):
    row_peers = [(lax.rem(me_r + j, n_rows), me_g) for j in range(1, n_rows)]
    grp_peers = [(me_r, lax.rem(me_g + j, n_grp)) for j in range(1, n_grp)]
    return row_peers, grp_peers


def forward_kernel(
    n_rows,
    total_pixels,
    f,
    dw,
    weight,
    col_sum,
    pool_weight,
    proj,
    pre_out,
    proj_out,
    pool_out,
    pooled_out,
    dep,
    to_mate,
    from_mate,
    to_x,
    from_x,
    sums,
    parts,
    projs,
    big_send,
    big_recv,
    sum_send,
    sum_recv,
    part_send,
    part_recv,
    proj_send,
    proj_recv,
):
    me_r, me_g = lax.axis_index("rows"), lax.axis_index("grp")
    row_peers, grp_peers = places_of(n_rows, 4, me_r, me_g)
    greet(row_peers + grp_peers)
    height = f.shape[0] - 2 * MARGIN
    width = f.shape[1]
    channels = f.shape[2]
    hold = weight.shape[2]
    quarter_rows = height // 4
    mate = me_g + 1 - 2 * lax.rem(me_g, 2)
    x_peer = lax.rem(me_g + 2, 4)
    diag = lax.rem(mate + 2, 4)

    sums[me_r] = col_sum[...]
    sum_copies = []
    for j, (pr, pg) in enumerate(row_peers):
        copy = remote(col_sum, sums.at[me_r], sum_send.at[j], sum_recv.at[j], pr, pg)
        copy.start()
        sum_copies.append(copy)
    projs[me_g] = proj[...]
    proj_copies = []
    for j, (pr, pg) in enumerate(grp_peers):
        copy = remote(proj, projs.at[me_g], proj_send.at[j], proj_recv.at[j], pr, pg)
        copy.start()
        proj_copies.append(copy)

    column = lax.broadcasted_iota(jnp.int32, (width, 128), 0)

    def quarter(q, put):
        def pair(p, carry):
            for i in range(2):
                h = q * quarter_rows + p * 2 + i + MARGIN

                def chunk(cc, inner):
                    ch = pl.ds(pl.multiple_of(cc * 128, 128), 128)
                    mid = f[h, :, ch].astype(F32)
                    for r, rate in enumerate(RATES):
                        taps = [f[h - rate, :, ch].astype(F32), mid, f[h + rate, :, ch].astype(F32)]
                        sides = []
                        for b in range(3):
                            at = r * 9 + b
                            sides.append(
                                dw[at : at + 1, ch] * taps[0]
                                + dw[at + 3 : at + 4, ch] * taps[1]
                                + dw[at + 6 : at + 7, ch] * taps[2]
                            )
                        left = jnp.where(column >= rate, pltpu.roll(sides[0], rate, 0), 0.0)
                        right = jnp.where(
                            column < width - rate, pltpu.roll(sides[2], width - rate, 0), 0.0
                        )
                        dep[r, i * width : (i + 1) * width, ch] = (left + sides[1] + right).astype(
                            BF16
                        )
                    return inner

                lax.fori_loop(0, channels // 128, chunk, 0)
            at_row = pl.ds(pl.multiple_of(p * 2 * width, 2 * width), 2 * width)
            plain = f[pl.ds(q * quarter_rows + p * 2 + MARGIN, 2)].reshape(2 * width, channels)
            for k in range(4):
                lhs = plain if k == 0 else dep[k - 1]
                put(at_row, k, jnp.dot(lhs, weight[k], preferred_element_type=F32))
            return carry

        lax.fori_loop(0, quarter_rows // 2, pair, 0)

    def put_mate(slot):
        def put(at_row, k, value):
            to_mate[slot, at_row, k * hold : (k + 1) * hold] = value.astype(BF16)

        return put

    def put_own(at_row, k, value):
        pre_out[at_row, k * hold : (k + 1) * hold] = value

    quarter(diag, put_mate(0))
    first = remote(
        to_mate.at[0], from_mate.at[0], big_send.at[0], big_recv.at[0], me_r, mate
    )
    first.start()

    quarter(x_peer, put_own)
    first.wait()
    step = 2 * width
    count = pre_out.shape[0] // step
    x_copies = []
    for p in range(count):
        span = slice(p * step, (p + 1) * step)
        to_x[span] = (pre_out[span] + from_mate[0, span].astype(F32)).astype(BF16)
        copy = remote(
            to_x.at[span], from_x.at[span], big_send.at[2 + p], big_recv.at[2 + p], me_r, x_peer
        )
        copy.start()
        x_copies.append(copy)

    for copy in sum_copies:
        copy.wait()
    pooled = sums[0]
    for j in range(1, n_rows):
        pooled = pooled + sums[j]
    pooled = pooled / total_pixels
    pooled_out[...] = pooled
    parts[me_g] = jnp.dot(
        pooled,
        pool_weight[...].astype(F32),
        precision=lax.Precision.HIGHEST,
        preferred_element_type=F32,
    )
    part_copies = []
    for j, (pr, pg) in enumerate(grp_peers):
        copy = remote(
            parts.at[me_g], parts.at[me_g], part_send.at[j], part_recv.at[j], pr, pg
        )
        copy.start()
        part_copies.append(copy)

    quarter(mate, put_mate(1))
    second = remote(
        to_mate.at[1], from_mate.at[1], big_send.at[1], big_recv.at[1], me_r, mate
    )
    second.start()
    quarter(me_g, put_own)

    for copy in part_copies:
        copy.wait()
    pool_out[...] = parts[0] + parts[1] + parts[2] + parts[3]
    for copy in proj_copies:
        copy.wait()
    proj_out[...] = projs[...]
    second.wait()
    for p in range(count):
        span = slice(p * step, (p + 1) * step)
        x_copies[p].wait()
        pre_out[span] = (
            pre_out[span] + from_mate[1, span].astype(F32) + from_x[span].astype(F32)
        )


def gather_kernel(
    grad, proj, small, grad_out, proj_out, small_out, slots, proj_slots, small_slots,
    big_send, big_recv, proj_send, proj_recv, small_send, small_recv,
):
    me_r, me_g = lax.axis_index("rows"), lax.axis_index("grp")
    grp_peers = [(me_r, lax.rem(me_g + j, 4)) for j in range(1, 4)]
    greet(grp_peers)
    mate = me_g + 1 - 2 * lax.rem(me_g, 2)
    x_peer = lax.rem(me_g + 2, 4)
    diag = lax.rem(mate + 2, 4)
    pieces = 4
    step = grad.shape[0] // pieces
    spans = [slice(p * step, (p + 1) * step) for p in range(pieces)]
    crossing = []
    for p, span in enumerate(spans):
        copy = remote(
            grad.at[span], slots.at[1, span], big_send.at[1 + p], big_recv.at[1 + p], me_r, x_peer
        )
        copy.start()
        crossing.append(copy)
    near = remote(grad, slots.at[0], big_send.at[0], big_recv.at[0], me_r, mate)
    near.start()
    others = []
    for j, (pr, pg) in enumerate(grp_peers):
        one = remote(proj.at[pg], proj_slots.at[j], proj_send.at[j], proj_recv.at[j], pr, pg)
        two = remote(small, small_slots.at[me_g], small_send.at[j], small_recv.at[j], pr, pg)
        one.start()
        two.start()
        others += [one, two]
    small_slots[me_g] = small[...]
    grad_out[me_g] = grad[...]
    near.wait()
    grad_out[mate] = slots[0]
    passing = []
    for p, span in enumerate(spans):
        crossing[p].wait()
        copy = remote(
            slots.at[1, span],
            slots.at[2, span],
            big_send.at[1 + pieces + p],
            big_recv.at[1 + pieces + p],
            me_r,
            mate,
        )
        copy.start()
        passing.append(copy)
    grad_out[x_peer] = slots[1]
    for copy in others:
        copy.wait()
    proj_out[...] = (
        proj[me_g] + proj_slots[0] + proj_slots[1] + proj_slots[2]
    )
    small_out[...] = small_slots[0] + small_slots[1] + small_slots[2] + small_slots[3]
    for copy in passing:
        copy.wait()
    grad_out[diag] = slots[2]


def reduce_kernel(n_rows, terms, out, landed, total, gathered, s_send, s_recv, g_send, g_recv):
    me_r, me_g = lax.axis_index("rows"), lax.axis_index("grp")
    row_peers = [(lax.rem(me_r + j, n_rows), me_g) for j in range(1, n_rows)]
    greet(row_peers)
    copies = []
    for j, (pr, pg) in enumerate(row_peers):
        copy = remote(terms.at[pr], landed.at[me_r], s_send.at[j], s_recv.at[j], pr, pg)
        copy.start()
        copies.append(copy)
    landed[me_r] = terms[me_r]
    for copy in copies:
        copy.wait()
    value = landed[0].astype(F32)
    for j in range(1, n_rows):
        value = value + landed[j].astype(F32)
    total[...] = value.astype(BF16)
    copies = []
    for j, (pr, pg) in enumerate(row_peers):
        copy = remote(total, gathered.at[me_r], g_send.at[j], g_recv.at[j], pr, pg)
        copy.start()
        copies.append(copy)
    gathered[me_r] = total[...]
    for copy in copies:
        copy.wait()
    out[...] = gathered[...].astype(F32)


def params(number):
    return pltpu.CompilerParams(
        collective_id=number, has_side_effects=True, vmem_limit_bytes=VMEM_LIMIT
    )


def dma(count):
    return pltpu.SemaphoreType.DMA((count,))


def halo(block, axis, width):
    count = lax.axis_size(axis)
    forward = [(i, i + 1) for i in range(count - 1)]
    backward = [(target, source) for source, target in forward]
    low = lax.ppermute(block[block.shape[0] - width :], axis, forward)
    high = lax.ppermute(block[:width], axis, backward)
    return jnp.concatenate([low, block, high], axis=0)


def slide(block, shift):
    if shift == 0:
        return block
    width = block.shape[1]
    if shift > 0:
        return jnp.pad(block[:, : width - shift], ((0, 0), (shift, 0), (0, 0)))
    return jnp.pad(block[:, -shift:], ((0, 0), (0, -shift), (0, 0)))


def per_device(
    features, depth_weight, branch_weight, pool_weight, proj_weight, class_weight, labels
):
    height, width, channels = features.shape
    n_rows = lax.axis_size("rows")
    me_g = lax.axis_index("grp")
    hold = branch_weight.shape[2]
    own_hold = proj_weight.shape[1]
    classes = class_weight.shape[1]
    total_pixels = height * n_rows * width
    own = height * width // 4
    padded = halo(features, "rows", MARGIN)
    col_sum = jnp.sum(features.astype(F32), axis=(0, 1))
    dw = depth_weight.reshape(27, channels)

    pre, projs, pool_pre8, pooled8 = pl.pallas_call(
        functools.partial(forward_kernel, n_rows, total_pixels),
        out_shape=(
            jax.ShapeDtypeStruct((own, 4 * hold), F32),
            jax.ShapeDtypeStruct((4,) + proj_weight.shape, BF16),
            jax.ShapeDtypeStruct((8, hold), F32),
            jax.ShapeDtypeStruct((8, channels), F32),
        ),
        in_specs=[vspec()] * 6,
        out_specs=(vspec(),) * 4,
        scratch_shapes=[
            pltpu.VMEM((3, 2 * width, channels), BF16),
            pltpu.VMEM((2, own, 4 * hold), BF16),
            pltpu.VMEM((2, own, 4 * hold), BF16),
            pltpu.VMEM((own, 4 * hold), BF16),
            pltpu.VMEM((own, 4 * hold), BF16),
            pltpu.VMEM((n_rows, 8, channels), F32),
            pltpu.VMEM((4, 8, hold), F32),
            pltpu.VMEM((4,) + proj_weight.shape, BF16),
            dma(2 + height // 8),
            dma(2 + height // 8),
            dma(n_rows - 1),
            dma(n_rows - 1),
            dma(3),
            dma(3),
            dma(3),
            dma(3),
        ],
        compiler_params=params(0),
    )(
        padded,
        dw,
        branch_weight,
        jnp.broadcast_to(col_sum[None], (8, channels)),
        pool_weight,
        proj_weight,
    )
    pooled = pooled8[0]
    pool_pre = pool_pre8[0]
    proj_all = projs.transpose(1, 0, 2, 3).reshape(5, hold, hold)
    proj_main = proj_all[:4].reshape(4 * hold, hold)

    branch_out = jnp.maximum(pre, 0.0).astype(BF16)
    pool_out = jnp.maximum(pool_pre, 0.0).astype(BF16)
    pool_term = jnp.sum(pool_out.astype(F32)[:, None] * proj_all[4].astype(F32), axis=0)
    mixed = jnp.dot(branch_out, proj_main, preferred_element_type=F32) + pool_term[None, :]
    hidden = jnp.maximum(mixed, 0.0).astype(BF16)
    logits = jnp.einsum("pc,ck->kp", hidden, class_weight, preferred_element_type=F32)
    expo = jnp.exp(logits)
    soft = expo / jnp.sum(expo, axis=0, keepdims=True)
    label_row = lax.dynamic_slice_in_dim(labels.reshape(-1), me_g * own, own)
    onehot = (lax.broadcasted_iota(jnp.int32, (classes, own), 0) == label_row[None, :]).astype(F32)
    valid = (label_row < classes).astype(F32)
    grad_logit = ((soft - onehot) * valid[None, :] / math.sqrt(total_pixels)).astype(BF16)
    class_part = jnp.einsum("pc,kp->kc", hidden, grad_logit, preferred_element_type=F32)
    back_hidden = jnp.einsum("ck,kp->pc", class_weight, grad_logit, preferred_element_type=F32)
    grad_mixed = (back_hidden * (mixed > 0)).astype(BF16)
    col_part = jnp.sum(grad_mixed.astype(F32), axis=0)
    back_pre = jnp.einsum("pd,cd->pc", grad_mixed, proj_main, preferred_element_type=F32)
    grad_pre = (back_pre * (pre > 0)).astype(BF16)
    proj_part = jnp.einsum("pc,pd->cd", branch_out, grad_mixed, preferred_element_type=F32)
    proj_part = (
        proj_part.reshape(4, 4, own_hold, hold).transpose(1, 0, 2, 3).reshape(4, hold, hold)
    )
    small_rows = -(-(classes + 1) // 8) * 8
    small = jnp.concatenate(
        [class_part, col_part[None], jnp.zeros((small_rows - classes - 1, hold), F32)], axis=0
    )

    pieces = 4
    grad_all, proj_sum, small_sum = pl.pallas_call(
        gather_kernel,
        out_shape=(
            jax.ShapeDtypeStruct((4, own, 4 * hold), BF16),
            jax.ShapeDtypeStruct((hold, hold), F32),
            jax.ShapeDtypeStruct((small_rows, hold), F32),
        ),
        in_specs=[vspec()] * 3,
        out_specs=(vspec(),) * 3,
        scratch_shapes=[
            pltpu.VMEM((3, own, 4 * hold), BF16),
            pltpu.VMEM((3, hold, hold), F32),
            pltpu.VMEM((4, small_rows, hold), F32),
            dma(1 + 2 * pieces),
            dma(1 + 2 * pieces),
            dma(3),
            dma(3),
            dma(3),
            dma(3),
        ],
        compiler_params=params(1),
    )(grad_pre, proj_part, small)

    grad_all = grad_all.reshape(height, width, 4 * hold)
    pixels = height * width

    def product(shift, columns):
        window = padded[MARGIN + shift : MARGIN + shift + height].reshape(pixels, channels)
        return jnp.einsum(
            "pc,pd->cd", window, columns.reshape(pixels, -1), preferred_element_type=F32
        )

    slid = []
    for r, rate in enumerate(RATES):
        part = grad_all[:, :, (r + 1) * hold : (r + 2) * hold]
        slid.append(
            jnp.concatenate([slide(part, (b - 1) * rate) for b in range(3)], axis=2)
        )
    branch_rows = [product(0, grad_all[:, :, :hold])]
    depth_rows = []
    for r, rate in enumerate(RATES):
        branch_sum = jnp.zeros((channels, hold), F32)
        for a in range(3):
            g = product((a - 1) * rate, slid[r])
            for b in range(3):
                term = g[:, b * hold : (b + 1) * hold]
                branch_sum = branch_sum + depth_weight[r, a, b][:, None] * term
                depth_rows.append(jnp.sum(term * branch_weight[r + 1].astype(F32), axis=1))
        branch_rows.append(branch_sum)
    depth_part = jnp.stack(depth_rows)

    terms = jnp.concatenate(
        branch_rows + [depth_part.reshape(-1, hold), proj_sum, small_sum], axis=0
    ).astype(BF16)
    used = terms.shape[0]
    span = -(-used // (n_rows * 16)) * 16
    terms = jnp.pad(terms, ((0, span * n_rows - used), (0, 0))).reshape(n_rows, span, hold)
    full = pl.pallas_call(
        functools.partial(reduce_kernel, n_rows),
        out_shape=jax.ShapeDtypeStruct((n_rows, span, hold), F32),
        in_specs=[vspec()],
        out_specs=vspec(),
        scratch_shapes=[
            pltpu.VMEM((n_rows, span, hold), BF16),
            pltpu.VMEM((span, hold), BF16),
            pltpu.VMEM((n_rows, span, hold), BF16),
            dma(n_rows - 1),
            dma(n_rows - 1),
            dma(n_rows - 1),
            dma(n_rows - 1),
        ],
        compiler_params=params(2),
    )(terms)
    full = full.reshape(n_rows * span, hold)
    at = 4 * channels
    grad_branch = full[:at].reshape(4, channels, hold)
    depth_len = 27 * channels // hold
    grad_depth = full[at : at + depth_len].reshape(3, 3, 3, channels)
    at += depth_len
    proj_main_grad = full[at : at + hold].reshape(4, own_hold, hold)
    at += hold
    grad_class = full[at : at + classes].T
    col_total = full[at + classes]
    back_pool = jnp.sum(proj_all[4].astype(F32) * col_total[None, :], axis=1)
    grad_poolpre = (back_pool * (pool_pre > 0)).astype(BF16)
    grad_pool = pooled[:, None] * grad_poolpre.astype(F32)[None, :]
    own_pool = lax.dynamic_slice_in_dim(pool_out, me_g * own_hold, own_hold)
    pool_proj = own_pool.astype(F32)[:, None] * col_total[None, :]
    grad_proj = jnp.concatenate([proj_main_grad, pool_proj[None]], axis=0)
    return (grad_branch, grad_depth, grad_pool, grad_proj, grad_class)


def solution(mesh):
    return jax.shard_map(
        per_device,
        mesh=mesh,
        in_specs=(
            P("rows", None, "grp"),
            P(None, None, None, "grp"),
            P(None, "grp", None),
            P("grp", None),
            P(None, "grp", None),
            P(),
            P("rows", None),
        ),
        out_specs=(
            P(None, "grp", None),
            P(None, None, None, "grp"),
            P("grp", None),
            P(None, "grp", None),
            P(),
        ),
        check_vma=False,
    )
```

time: 933 us -> 412 us (0.44)
  waiting for transfers between devices: 496 us -> 85.3 us
  Pallas kernels: 0 us -> 175 us
  blocking collectives: 113 us -> 0 us
  matrix products: 118 us -> 50.2 us
  other arithmetic: 88.6 us -> 27.7 us
  local copies, waits for them, and re-layouts: 86.1 us -> 59.6 us
  between operations: 16 us -> 1.55 us
    psum x3 -> x0, waiting for transfers between devices: 236 us -> none  [the longest x2 167 us: per_device(): lax.psum((branch_part, depth_part, proj_part, class_part), 'rows')]
    unnamed x8 -> x0, waiting for transfers between devices: 221 us -> none
    pallas_call x0 -> x3, Pallas kernels: none -> 175 us  [the longest x1 66.5 us: per_device(): pl.pallas_call(functools.partial(reduce_kernel, n_rows), out_shape=jax.Sh...]
    psum x1 -> x0, blocking collectives: 105 us -> none  [per_device(): pooled = lax.psum(column_sum, 'rows') / total_pixels]
    ppermute x2, waiting for transfers between devices: 0.01 us -> 85.3 us  [the longest x1 50.5 us: halo(): high = lax.ppermute(block[:width], axis, backward)]
    convert_element_type x7 -> x4, other arithmetic: 76.2 us -> 2.34 us  [the longest x1 0.78 us: per_device(): pool_out = jnp.maximum(pool_pre, 0.0).astype(BF16)]
    dot_general x20 -> x16, matrix products: 118 us -> 50.2 us  [the longest x10 44.6 us: product(): jnp.einsum('pc,pd->cd', window, columns.reshape(pixels, -1), preferred_el...]
    all_gather x1 -> x0, waiting for transfers between devices: 39.3 us -> none  [per_device(): lax.all_gather(own_grad, 'grp', axis=2, tiled=True)]
  transfers between devices with their start and end apart: 8 -> 2, of which waited for: 5 -> 2; matrix products, arithmetic and copies ran while one was open for 13% -> 3% of each run, Pallas kernels for 0% -> 0%
where the time goes in v1:
time: 412 us; the launch traced here: 406 us
  Pallas kernels  175 us (42%)
  waiting for transfers between devices  85.3 us (21%)
  local copies, waits for them, and re-layouts  59.6 us (14%)
  matrix products  50.2 us (12%)
  other arithmetic  27.7 us (7%)
  starting transfers between devices  6.88 us (2%)
    pallas_call x1, Pallas kernels, per_device(): pl.pallas_call(functools.partial(reduce_kernel, n_rows), out_shape=jax.Sh...  66.5 us
    pallas_call x1, Pallas kernels, per_device(): pl.pallas_call(functools.partial(forward_kernel, n_rows, total_pixels), o...  55.1 us
    pallas_call x1, Pallas kernels, per_device(): pl.pallas_call(gather_kernel, out_shape=(jax.ShapeDtypeStruct((4, own, 4...  53.2 us
    ppermute x1, waiting for transfers between devices, halo(): high = lax.ppermute(block[:width], axis, backward)  50.5 us
    dot_general x10, matrix products, product(): jnp.einsum('pc,pd->cd', window, columns.reshape(pixels, -1), preferred_el...  44.6 us
    ppermute x1, waiting for transfers between devices, halo(): low = lax.ppermute(block[block.shape[0] - width:], axis, forward)  34.8 us
    unnamed x81, local copies, waits for them, and re-layouts  10.1 us
  transfers between devices with their start and end apart: 2, of which 2 were waited for; matrix products, arithmetic and copies ran while one was open for 3% of the time, Pallas kernels for 0%

profile of v1, /device:TPU:29, one launch (start us, length us, event | category | flops | bytes accessed | tf_op | source)
XLA Modules:
  0.0 406.0 jit_solution(11065435489544024318)
XLA Ops:
  0.7 5.3 %fusion.97 = (bf16[18,128,512]{2,1,0:T(8,128)(2,1)}, bf16[18,128,512]{2,1,0:T(8,128)(2,1)}) fusion(bf16[24,128,512]{2,1,0:T(8,128)(2,1)} %param.7), kind=kLoop, calls=%fused_computation.140 | loop fusion | bytes 9437184 | tf_op jit(solution)/shard_map/slice | solution.py:312
  6.0 1.4 collective-permute-start
  7.4 5.5 %collective-permute-start.1 = (bf16[18,128,512]{2,1,0:T(8,128)(2,1)}, bf16[18,128,512]{2,1,0:T(8,128)(2,1)}, u32[]{:S(2)}, u32[]{:S(2)}) collective-permute-start(bf16[18,128,512]{2,1,0:T(8,128)(2,1)} %get-tuple-element.76), channel_id=1, source_target_pairs={{4,0},{8,4},{12,8},{16,12},{20,16},{24,20},{28,24},{5,1},{9,5},{13... | collective-permute-start | bytes 7077896 | tf_op jit(solution)/shard_map/ppermute | solution.py:313
  12.8 2.8 copy.52
  16.3 2.0 fusion.98
  18.3 1.1 copy.122
  19.4 1.8 copy.121
  21.2 1.8 copy.120
  25.6 34.8 %collective-permute-done = bf16[18,128,512]{2,1,0:T(8,128)(2,1)} collective-permute-done((bf16[18,128,512]{2,1,0:T(8,128)(2,1)}, bf16[18,128,512]{2,1,0:T(8,128)(2,1)}, u32[]{:S(2)}, u32[]{:S(2)}) %collective-permute-start) | collective-permute-done | bytes 2359328 | tf_op jit(solution)/shard_map/ppermute | solution.py:312
  60.4 50.5 %collective-permute-done.1 = bf16[18,128,512]{2,1,0:T(8,128)(2,1)} collective-permute-done((bf16[18,128,512]{2,1,0:T(8,128)(2,1)}, bf16[18,128,512]{2,1,0:T(8,128)(2,1)}, u32[]{:S(2)}, u32[]{:S(2)}) %collective-permute-start.1) | collective-permute-done | bytes 2359328 | tf_op jit(solution)/shard_map/ppermute | solution.py:313
  110.9 6.1 %pad_maximum_fusion.f = bf16[60,128,512]{2,1,0:T(8,128)(2,1)} fusion(bf16[18,128,512]{2,1,0:T(8,128)(2,1)} %collective-permute-done.1, bf16[24,128,512]{2,1,0:T(8,128)(2,1)S(1)} %copy-done.2, bf16[18,128,512]{2,1,0:T(8,128)(2,1)} %collective-permute-done), kind=kLoop, calls=%fused_computation.8 | loop fusion | flops 7864320 | bytes 15728640 | tf_op jit(solution)/shard_map/concatenate | solution.py:314
  117.7 55.1 %shard_map.110 = (f32[768,1024]{1,0:T(8,128)}, bf16[4,5,64,256]{3,2,1,0:T(8,128)(2,1)}, f32[8,256]{1,0:T(8,128)}, f32[8,512]{1,0:T(8,128)}) custom-call(bf16[60,128,512]{2,1,0:T(8,128)(2,1)} %pad_maximum_fusion.f, f32[27,512]{1,0:T(8,128)} %reshape.189.dw, bf16[4,512,256]{2,1,0:T(8,128)(2,1)} %weight.1, f32[8,512]{1,0:T(8,128)} %broadcast_in_dim.6.col_sum, ...), custom_call_target="tpu_custom_call" | custom-call | tf_op jit(solution)/shard_map/pallas_call | solution.py:341
  173.6 1.2 slice.375
  174.8 1.0 fusion.64
  175.9 2.5 convolution_add_fusion
  179.8 1.8 select_convert_fusion.grad
  181.6 1.1 copy.49
  183.3 53.2 %shard_map.111 = (bf16[4,768,1024]{2,1,0:T(8,128)(2,1)}, f32[256,256]{1,0:T(8,128)}, f32[16,256]{1,0:T(8,128)}) custom-call(bf16[768,1024]{1,0:T(8,128)(2,1)} %select_convert_fusion.grad, f32[4,256,256]{2,1,0:T(8,128)} %bitcast.166, f32[16,256]{1,0:T(8,128)} %maximum_maximum_fusion.small), custom_call_target="tpu_custom_call" | custom-call | tf_op jit(solution)/shard_map/pallas_call | solution.py:411
  236.5 3.3 fusion.33
  239.8 2.4 fusion.94
  242.2 2.6 fusion.95
  244.7 1.1 fusion.96
  245.8 2.5 fusion.93
  248.5 1.0 copy-done.20
  249.4 3.8 convolution_bitcast_fusion.2
  253.2 4.4 %copy.59 = bf16[18,128,512]{1,2,0:T(8,128)(2,1)} copy(bf16[18,128,512]{2,1,0:T(8,128)(2,1)} %collective-permute-done.1) | data formatting | bytes 4718592 | tf_op jit(solution)/shard_map/ppermute | solution.py:313
  257.7 7.2 %fusion.23 = f32[512,768]{0,1:T(8,128)} fusion(bf16[18,128,512]{1,2,0:T(8,128)(2,1)} %copy.59, bf16[24,128,512]{1,2,0:T(8,128)(2,1)} %copy.52, bf16[24,122,256]{2,1,0:T(8,128)(2,1)} %copy-done.22, bf16[24,122,256]{2,1,0:T(8,128)(2,1)} %copy-done.21, bf16[24,128,256]{2,1,0:T(8,128)(2,1)} %copy-done.20), kind=kOutput, calls=%fused_computation.61 | convolution fusion | flops 2450522112 | bytes 11649024 | tf_op jit(solution)/shard_map/pc,pd->cd/dot_general | solution.py:439
  264.9 3.8 convolution_bitcast_fusion
  268.8 3.8 fusion.25
  272.6 4.4 %copy.51 = bf16[18,128,512]{1,2,0:T(8,128)(2,1)} copy(bf16[18,128,512]{2,1,0:T(8,128)(2,1)} %collective-permute-done) | data formatting | bytes 4718592 | tf_op jit(solution)/shard_map/ppermute | solution.py:312
  277.1 7.3 %fusion.20 = f32[512,768]{0,1:T(8,128)} fusion(bf16[24,128,512]{1,2,0:T(8,128)(2,1)} %copy.52, bf16[18,128,512]{1,2,0:T(8,128)(2,1)} %copy.51, bf16[24,122,256]{2,1,0:T(8,128)(2,1)} %copy-done.22, bf16[24,122,256]{2,1,0:T(8,128)(2,1)} %copy-done.21, bf16[24,128,256]{2,1,0:T(8,128)(2,1)} %copy-done.20), kind=kOutput, calls=%fused_computation.58 | convolution fusion | flops 2450522112 | bytes 11649024 | tf_op jit(solution)/shard_map/pc,pd->cd/dot_general | solution.py:439
  284.4 3.8 fusion.22
  288.2 3.8 fusion.21
  292.0 3.8 fusion.24
  295.8 4.0 convolution_bitcast_fusion.1
  301.7 3.2 fusion.45
  309.0 3.0 fusion.54
  313.5 1.5 stack.139
  315.8 3.1 add_convert_fusion.2
  319.6 2.0 add_convert_fusion.1
  321.6 1.3 add_convert_fusion
  322.9 2.4 concatenate.39
  326.1 1.1 pad.34.clone
  327.2 66.5 %shard_map.112 = f32[8,304,256]{2,1,0:T(8,128)} custom-call(bf16[8,304,256]{2,1,0:T(8,128)(2,1)} %bitcast.163), custom_call_target="tpu_custom_call" | custom-call | tf_op jit(solution)/shard_map/pallas_call | solution.py:468
  394.5 1.3 slice_bitcast_fusion
  396.6 1.0 slice.417
  397.6 3.0 slice.414
  401.4 1.0 fusion.65
  (136 shorter events, 22.0 us)
Async XLA Ops:
  0.6 177.7 %copy-start = (bf16[256,11]{0,1:T(8,128)(2,1)S(1)}, bf16[256,11]{0,1:T(8,128)(2,1)}, u32[]{:S(2)}) copy-start(bf16[256,11]{0,1:T(8,128)(2,1)} %param.12) | copy-start | bytes 16900
  0.6 12.2 %copy-start.2 = (bf16[24,128,512]{2,1,0:T(8,128)(2,1)S(1)}, bf16[24,128,512]{2,1,0:T(8,128)(2,1)}, u32[]{:S(2)}) copy-start(bf16[24,128,512]{2,1,0:T(8,128)(2,1)} %param.7) | copy-start | bytes 9437188
  6.0 9.7 %copy-start.29 = (f32[3,3,3,512]{3,2,1,0:T(4,128)S(1)}, f32[3,3,3,512]{3,2,1,0:T(4,128)}, u32[]{:S(2)}) copy-start(f32[3,3,3,512]{3,2,1,0:T(4,128)} %param.8) | copy-start | bytes 165892
  6.0 54.4 %collective-permute-start = (bf16[18,128,512]{2,1,0:T(8,128)(2,1)}, bf16[18,128,512]{2,1,0:T(8,128)(2,1)}, u32[]{:S(2)}, u32[]{:S(2)}) collective-permute-start(bf16[18,128,512]{2,1,0:T(8,128)(2,1)} %get-tuple-element.75), channel_id=1, source_target_pairs={{0,4},{4,8},{8,12},{12,16},{16,20},{20,24},{24,28},{1,5},{5,9},{9,... | collective-permute-start | bytes 7077896 | tf_op jit(solution)/shard_map/ppermute | solution.py:312
  7.4 103.6 %collective-permute-start.1 = (bf16[18,128,512]{2,1,0:T(8,128)(2,1)}, bf16[18,128,512]{2,1,0:T(8,128)(2,1)}, u32[]{:S(2)}, u32[]{:S(2)}) collective-permute-start(bf16[18,128,512]{2,1,0:T(8,128)(2,1)} %get-tuple-element.76), channel_id=1, source_target_pairs={{4,0},{8,4},{12,8},{16,12},{20,16},{24,20},{28,24},{5,1},{9,5},{13... | collective-permute-start | bytes 7077896 | tf_op jit(solution)/shard_map/ppermute | solution.py:313
  173.6 5.6 %copy-start.4 = (f32[768,1024]{1,0:T(8,128)S(1)}, f32[768,1024]{1,0:T(8,128)}, u32[]{:S(2)}) copy-start(f32[768,1024]{1,0:T(8,128)} %get-tuple-element.12) | copy-start | bytes 9437188
  236.5 3.3 copy-start.3
  245.8 2.5 copy-start.21
  245.8 2.6 copy-start.22
  248.3 1.1 copy-start.20
  257.7 7.3 %copy-start.18 = (bf16[24,128,256]{2,1,0:T(8,128)(2,1)S(1)}, bf16[24,128,256]{2,1,0:T(8,128)(2,1)}, u32[]{:S(2)}) copy-start(bf16[24,128,256]{2,1,0:T(8,128)(2,1)} %get-tuple-element.66) | copy-start | bytes 4718596
  257.7 7.2 %copy-start.25 = (bf16[24,110,256]{2,1,0:T(8,128)(2,1)S(1)}, bf16[24,110,256]{2,1,0:T(8,128)(2,1)}, u32[]{:S(2)}) copy-start(bf16[24,110,256]{2,1,0:T(8,128)(2,1)} %get-tuple-element.69) | copy-start | bytes 4055044
  257.7 7.2 %copy-start.27 = (bf16[24,110,256]{2,1,0:T(8,128)(2,1)S(1)}, bf16[24,110,256]{2,1,0:T(8,128)(2,1)}, u32[]{:S(2)}) copy-start(bf16[24,110,256]{2,1,0:T(8,128)(2,1)} %get-tuple-element.70) | copy-start | bytes 4055044
  264.9 3.8 copy-start.12
  264.9 3.8 copy-start.14
  277.0 7.3 %copy-start.13 = (bf16[24,128,512]{1,2,0:T(8,128)(2,1)S(1)}, bf16[24,128,512]{1,2,0:T(8,128)(2,1)}, u32[]{:S(2)}) copy-start(bf16[24,128,512]{1,2,0:T(8,128)(2,1)} %copy.52) | copy-start | bytes 9437188
  277.0 7.3 %copy-start.16 = (bf16[18,128,512]{1,2,0:T(8,128)(2,1)S(1)}, bf16[18,128,512]{1,2,0:T(8,128)(2,1)}, u32[]{:S(2)}) copy-start(bf16[18,128,512]{1,2,0:T(8,128)(2,1)} %copy.51) | copy-start | bytes 7077892
  277.1 7.3 %copy-start.19 = (bf16[24,128,256]{2,1,0:T(8,128)(2,1)S(1)}, bf16[24,128,256]{2,1,0:T(8,128)(2,1)}, u32[]{:S(2)}) copy-start(bf16[24,128,256]{2,1,0:T(8,128)(2,1)} %get-tuple-element.66) | copy-start | bytes 4718596
  277.1 7.3 %copy-start.26 = (bf16[24,110,256]{2,1,0:T(8,128)(2,1)S(1)}, bf16[24,110,256]{2,1,0:T(8,128)(2,1)}, u32[]{:S(2)}) copy-start(bf16[24,110,256]{2,1,0:T(8,128)(2,1)} %get-tuple-element.69) | copy-start | bytes 4055044
  277.1 7.3 %copy-start.28 = (bf16[24,110,256]{2,1,0:T(8,128)(2,1)S(1)}, bf16[24,110,256]{2,1,0:T(8,128)(2,1)}, u32[]{:S(2)}) copy-start(bf16[24,110,256]{2,1,0:T(8,128)(2,1)} %get-tuple-element.70) | copy-start | bytes 4055044
  284.4 3.8 copy-start.17
  284.4 3.8 copy-start.23
  284.4 3.8 copy-start.24
  288.2 3.8 copy-start.15
  295.8 4.0 copy-start.30
  301.7 10.9 %copy-start.5 = (f32[512,768]{0,1:T(8,128)S(1)}, f32[512,768]{0,1:T(8,128)}, u32[]{:S(2)}) copy-start(f32[512,768]{0,1:T(8,128)} %convolution_bitcast_fusion) | copy-start | bytes 4718596
  301.7 10.9 %copy-start.6 = (f32[512,768]{0,1:T(8,128)S(1)}, f32[512,768]{0,1:T(8,128)}, u32[]{:S(2)}) copy-start(f32[512,768]{0,1:T(8,128)} %fusion.25) | copy-start | bytes 4718596
  301.7 10.9 %copy-start.7 = (f32[512,768]{0,1:T(8,128)S(1)}, f32[512,768]{0,1:T(8,128)}, u32[]{:S(2)}) copy-start(f32[512,768]{0,1:T(8,128)} %fusion.22) | copy-start | bytes 4718596
  315.8 3.2 copy-start.9
  315.8 3.3 copy-start.10
  315.8 3.8 copy-start.11
  315.8 5.8 %copy-start.8 = (f32[512,768]{0,1:T(8,128)S(1)}, f32[512,768]{0,1:T(8,128)}, u32[]{:S(2)}) copy-start(f32[512,768]{0,1:T(8,128)} %fusion.22) | copy-start | bytes 4718596
  315.8 5.8 %copy-start.31 = (f32[1,1,1,512]{3,2,1,0:T(1,128)S(1)}, f32[1,1,1,512]{3,2,1,0:T(1,128)}, u32[]{:S(2)}) copy-start(f32[1,1,1,512]{3,2,1,0:T(1,128)} %get-tuple-element.80) | copy-start | bytes 6148
  315.8 5.8 %copy-start.32 = (f32[1,1,1,512]{3,2,1,0:T(1,128)S(1)}, f32[1,1,1,512]{3,2,1,0:T(1,128)}, u32[]{:S(2)}) copy-start(f32[1,1,1,512]{3,2,1,0:T(1,128)} %get-tuple-element.81) | copy-start | bytes 6148
  315.8 5.8 %copy-start.33 = (f32[1,1,1,512]{3,2,1,0:T(1,128)S(1)}, f32[1,1,1,512]{3,2,1,0:T(1,128)}, u32[]{:S(2)}) copy-start(f32[1,1,1,512]{3,2,1,0:T(1,128)} %get-tuple-element.82) | copy-start | bytes 6148
  315.8 5.8 %copy-start.34 = (f32[1,1,1,512]{3,2,1,0:T(1,128)S(1)}, f32[1,1,1,512]{3,2,1,0:T(1,128)}, u32[]{:S(2)}) copy-start(f32[1,1,1,512]{3,2,1,0:T(1,128)} %get-tuple-element.83) | copy-start | bytes 6148
  315.8 5.8 %copy-start.35 = (f32[1,1,1,512]{3,2,1,0:T(1,128)S(1)}, f32[1,1,1,512]{3,2,1,0:T(1,128)}, u32[]{:S(2)}) copy-start(f32[1,1,1,512]{3,2,1,0:T(1,128)} %get-tuple-element.84) | copy-start | bytes 6148
  315.8 5.8 %copy-start.36 = (f32[1,1,1,512]{3,2,1,0:T(1,128)S(1)}, f32[1,1,1,512]{3,2,1,0:T(1,128)}, u32[]{:S(2)}) copy-start(f32[1,1,1,512]{3,2,1,0:T(1,128)} %get-tuple-element.85) | copy-start | bytes 6148
  315.8 5.8 %copy-start.37 = (f32[1,1,1,512]{3,2,1,0:T(1,128)S(1)}, f32[1,1,1,512]{3,2,1,0:T(1,128)}, u32[]{:S(2)}) copy-start(f32[1,1,1,512]{3,2,1,0:T(1,128)} %get-tuple-element.86) | copy-start | bytes 6148
  327.2 78.6 %copy-start.1 = (bf16[256,11]{0,1:T(8,128)(2,1)S(1)}, bf16[256,11]{0,1:T(8,128)(2,1)}, u32[]{:S(2)}) copy-start(bf16[256,11]{0,1:T(8,128)(2,1)} %param.12) | copy-start | bytes 16900

commit v2 on v1

--- a/solution.py
+++ b/solution.py
@@ -47,17 +47,19 @@
 def forward_kernel(
     n_rows,
     total_pixels,
-    f,
+    features,
     dw,
     weight,
     col_sum,
     pool_weight,
     proj,
     pre_out,
+    f,
     proj_out,
     pool_out,
     pooled_out,
     dep,
+    cross,
     to_mate,
     from_mate,
     to_x,
@@ -65,8 +67,13 @@
     sums,
     parts,
     projs,
-    big_send,
-    big_recv,
+    local_sem,
+    halo_send,
+    halo_recv,
+    mate_send,
+    mate_recv,
+    x_send,
+    x_recv,
     sum_send,
     sum_recv,
     part_send,
@@ -76,7 +83,6 @@
 ):
     me_r, me_g = lax.axis_index("rows"), lax.axis_index("grp")
     row_peers, grp_peers = places_of(n_rows, 4, me_r, me_g)
-    greet(row_peers + grp_peers)
     height = f.shape[0] - 2 * MARGIN
     width = f.shape[1]
     channels = f.shape[2]
@@ -85,6 +91,51 @@
     mate = me_g + 1 - 2 * lax.rem(me_g, 2)
     x_peer = lax.rem(me_g + 2, 4)
     diag = lax.rem(mate + 2, 4)
+    greet(row_peers + grp_peers)
+
+    after, before = lax.rem(me_r + 1, n_rows), lax.rem(me_r + n_rows - 1, n_rows)
+    piece = MARGIN // 3
+    up, down = [], []
+    for t in range(3):
+        up.append(
+            remote(
+                features.at[pl.ds(height - piece * (t + 1), piece)],
+                f.at[pl.ds(MARGIN - piece * (t + 1), piece)],
+                halo_send.at[t],
+                halo_recv.at[t],
+                after,
+                me_g,
+            )
+        )
+        down.append(
+            remote(
+                features.at[pl.ds(piece * t, piece)],
+                f.at[pl.ds(MARGIN + height + piece * t, piece)],
+                halo_send.at[3 + t],
+                halo_recv.at[3 + t],
+                before,
+                me_g,
+            )
+        )
+    middle = pltpu.make_async_copy(features, f.at[pl.ds(MARGIN, height)], local_sem)
+    middle.start()
+    for t in range(3):
+
+        @pl.when(me_r < n_rows - 1)
+        def _():
+            up[t].start()
+
+        @pl.when(me_r > 0)
+        def _():
+            down[t].start()
+
+    @pl.when(me_r == 0)
+    def _():
+        f[pl.ds(0, MARGIN)] = jnp.zeros((MARGIN, width, channels), BF16)
+
+    @pl.when(me_r == n_rows - 1)
+    def _():
+        f[pl.ds(MARGIN + height, MARGIN)] = jnp.zeros((MARGIN, width, channels), BF16)
 
     sums[me_r] = col_sum[...]
     sum_copies = []
@@ -101,19 +152,22 @@
 
     column = lax.broadcasted_iota(jnp.int32, (width, 128), 0)
 
-    def quarter(q, put):
+    def quarter(q, k, put):
         def pair(p, carry):
-            for i in range(2):
-                h = q * quarter_rows + p * 2 + i + MARGIN
+            first_row = q * quarter_rows + p * 2 + MARGIN
+            if k == 0:
+                lhs = f[pl.ds(first_row, 2)].reshape(2 * width, channels)
+            else:
+                rate = RATES[k - 1]
 
                 def chunk(cc, inner):
                     ch = pl.ds(pl.multiple_of(cc * 128, 128), 128)
-                    mid = f[h, :, ch].astype(F32)
-                    for r, rate in enumerate(RATES):
-                        taps = [f[h - rate, :, ch].astype(F32), mid, f[h + rate, :, ch].astype(F32)]
+                    for i in range(2):
+                        h = first_row + i
+                        taps = [f[h + (a - 1) * rate, :, ch].astype(F32) for a in range(3)]
                         sides = []
                         for b in range(3):
-                            at = r * 9 + b
+                            at = (k - 1) * 9 + b
                             sides.append(
                                 dw[at : at + 1, ch] * taps[0]
                                 + dw[at + 3 : at + 4, ch] * taps[1]
@@ -123,50 +177,62 @@
                         right = jnp.where(
                             column < width - rate, pltpu.roll(sides[2], width - rate, 0), 0.0
                         )
-                        dep[r, i * width : (i + 1) * width, ch] = (left + sides[1] + right).astype(
+                        dep[i * width : (i + 1) * width, ch] = (left + sides[1] + right).astype(
                             BF16
                         )
                     return inner
 
                 lax.fori_loop(0, channels // 128, chunk, 0)
+                lhs = dep[...]
             at_row = pl.ds(pl.multiple_of(p * 2 * width, 2 * width), 2 * width)
-            plain = f[pl.ds(q * quarter_rows + p * 2 + MARGIN, 2)].reshape(2 * width, channels)
-            for k in range(4):
-                lhs = plain if k == 0 else dep[k - 1]
-                put(at_row, k, jnp.dot(lhs, weight[k], preferred_element_type=F32))
+            put(at_row, jnp.dot(lhs, weight[k], preferred_element_type=F32))
             return carry
 
         lax.fori_loop(0, quarter_rows // 2, pair, 0)
 
-    def put_mate(slot):
-        def put(at_row, k, value):
-            to_mate[slot, at_row, k * hold : (k + 1) * hold] = value.astype(BF16)
-
-        return put
-
-    def put_own(at_row, k, value):
-        pre_out[at_row, k * hold : (k + 1) * hold] = value
-
-    quarter(diag, put_mate(0))
-    first = remote(
-        to_mate.at[0], from_mate.at[0], big_send.at[0], big_recv.at[0], me_r, mate
-    )
-    first.start()
-
-    quarter(x_peer, put_own)
-    first.wait()
-    step = 2 * width
-    count = pre_out.shape[0] // step
-    x_copies = []
-    for p in range(count):
-        span = slice(p * step, (p + 1) * step)
-        to_x[span] = (pre_out[span] + from_mate[0, span].astype(F32)).astype(BF16)
-        copy = remote(
-            to_x.at[span], from_x.at[span], big_send.at[2 + p], big_recv.at[2 + p], me_r, x_peer
-        )
-        copy.start()
-        x_copies.append(copy)
-
+    seconds, crossings = [], []
+
+    def branch(k):
+        def put_mate(slot):
+            def put(at_row, value):
+                to_mate[k, slot, at_row] = value.astype(BF16)
+
+            return put
+
+        def put_cross(at_row, value):
+            cross[at_row] = value
+
+        def put_own(at_row, value):
+            pre_out[at_row, k * hold : (k + 1) * hold] = value
+
+        def to_core(slot):
+            copy = remote(
+                to_mate.at[k, slot],
+                from_mate.at[k, slot],
+                mate_send.at[2 * k + slot],
+                mate_recv.at[2 * k + slot],
+                me_r,
+                mate,
+            )
+            copy.start()
+            return copy
+
+        quarter(diag, k, put_mate(0))
+        first = to_core(0)
+        quarter(x_peer, k, put_cross)
+        first.wait()
+        to_x[k] = (cross[...] + from_mate[k, 0].astype(F32)).astype(BF16)
+        crossing = remote(
+            to_x.at[k], from_x.at[k], x_send.at[k], x_recv.at[k], me_r, x_peer
+        )
+        crossing.start()
+        crossings.append(crossing)
+        quarter(mate, k, put_mate(1))
+        seconds.append(to_core(1))
+        quarter(me_g, k, put_own)
+
+    middle.wait()
+    branch(0)
     for copy in sum_copies:
         copy.wait()
     pooled = sums[0]
@@ -187,27 +253,41 @@
         )
         copy.start()
         part_copies.append(copy)
-
-    quarter(mate, put_mate(1))
-    second = remote(
-        to_mate.at[1], from_mate.at[1], big_send.at[1], big_recv.at[1], me_r, mate
-    )
-    second.start()
-    quarter(me_g, put_own)
-
     for copy in part_copies:
         copy.wait()
     pool_out[...] = parts[0] + parts[1] + parts[2] + parts[3]
     for copy in proj_copies:
         copy.wait()
     proj_out[...] = projs[...]
-    second.wait()
-    for p in range(count):
-        span = slice(p * step, (p + 1) * step)
-        x_copies[p].wait()
-        pre_out[span] = (
-            pre_out[span] + from_mate[1, span].astype(F32) + from_x[span].astype(F32)
-        )
+
+    for k in range(1, 4):
+
+        @pl.when(me_r > 0)
+        def _():
+            up[k - 1].wait_recv()
+
+        @pl.when(me_r < n_rows - 1)
+        def _():
+            down[k - 1].wait_recv()
+
+        branch(k)
+
+    for k in range(4):
+        seconds[k].wait()
+        crossings[k].wait()
+        span = slice(k * hold, (k + 1) * hold)
+        pre_out[:, span] = (
+            pre_out[:, span] + from_mate[k, 1].astype(F32) + from_x[k].astype(F32)
+        )
+    for t in range(3):
+
+        @pl.when(me_r < n_rows - 1)
+        def _():
+            up[t].wait_send()
+
+        @pl.when(me_r > 0)
+        def _():
+            down[t].wait_send()
 
 
 def gather_kernel(
@@ -305,15 +385,6 @@
     return pltpu.SemaphoreType.DMA((count,))
 
 
-def halo(block, axis, width):
-    count = lax.axis_size(axis)
-    forward = [(i, i + 1) for i in range(count - 1)]
-    backward = [(target, source) for source, target in forward]
-    low = lax.ppermute(block[block.shape[0] - width :], axis, forward)
-    high = lax.ppermute(block[:width], axis, backward)
-    return jnp.concatenate([low, block, high], axis=0)
-
-
 def slide(block, shift):
     if shift == 0:
         return block
@@ -334,31 +405,37 @@
     classes = class_weight.shape[1]
     total_pixels = height * n_rows * width
     own = height * width // 4
-    padded = halo(features, "rows", MARGIN)
     col_sum = jnp.sum(features.astype(F32), axis=(0, 1))
     dw = depth_weight.reshape(27, channels)
 
-    pre, projs, pool_pre8, pooled8 = pl.pallas_call(
+    pre, padded, projs, pool_pre8, pooled8 = pl.pallas_call(
         functools.partial(forward_kernel, n_rows, total_pixels),
         out_shape=(
             jax.ShapeDtypeStruct((own, 4 * hold), F32),
+            jax.ShapeDtypeStruct((height + 2 * MARGIN, width, channels), BF16),
             jax.ShapeDtypeStruct((4,) + proj_weight.shape, BF16),
             jax.ShapeDtypeStruct((8, hold), F32),
             jax.ShapeDtypeStruct((8, channels), F32),
         ),
-        in_specs=[vspec()] * 6,
-        out_specs=(vspec(),) * 4,
+        in_specs=[pl.BlockSpec(memory_space=pl.ANY)] + [vspec()] * 5,
+        out_specs=(vspec(),) * 5,
         scratch_shapes=[
-            pltpu.VMEM((3, 2 * width, channels), BF16),
-            pltpu.VMEM((2, own, 4 * hold), BF16),
-            pltpu.VMEM((2, own, 4 * hold), BF16),
-            pltpu.VMEM((own, 4 * hold), BF16),
-            pltpu.VMEM((own, 4 * hold), BF16),
+            pltpu.VMEM((2 * width, channels), BF16),
+            pltpu.VMEM((own, hold), F32),
+            pltpu.VMEM((4, 2, own, hold), BF16),
+            pltpu.VMEM((4, 2, own, hold), BF16),
+            pltpu.VMEM((4, own, hold), BF16),
+            pltpu.VMEM((4, own, hold), BF16),
             pltpu.VMEM((n_rows, 8, channels), F32),
             pltpu.VMEM((4, 8, hold), F32),
             pltpu.VMEM((4,) + proj_weight.shape, BF16),
-            dma(2 + height // 8),
-            dma(2 + height // 8),
+            pltpu.SemaphoreType.DMA,
+            dma(6),
+            dma(6),
+            dma(8),
+            dma(8),
+            dma(4),
+            dma(4),
             dma(n_rows - 1),
             dma(n_rows - 1),
             dma(3),
@@ -368,7 +445,7 @@
         ],
         compiler_params=params(0),
     )(
-        padded,
+        features,
         dw,
         branch_weight,
         jnp.broadcast_to(col_sum[None], (8, channels)),

time: 412 us -> 349 us (0.85)
  Pallas kernels: 175 us -> 266 us
  waiting for transfers between devices: 85.3 us -> 0 us
  local copies, waits for them, and re-layouts: 59.6 us -> 25.9 us
  matrix products: 50.2 us -> 32.5 us
  other arithmetic: 27.7 us -> 17.8 us
  starting transfers between devices: 6.88 us -> 0 us
    pallas_call x1, Pallas kernels: 55.1 us -> 145 us  [per_device(): pl.pallas_call(functools.partial(forward_kernel, n_rows, total_pixels), o...]
    ppermute x2 -> x0, waiting for transfers between devices: 85.3 us -> none  [the longest x1 50.5 us: halo(): high = lax.ppermute(block[:width], axis, backward)]
    dot_general x10, matrix products: 44.6 us -> 26.9 us  [product(): jnp.einsum('pc,pd->cd', window, columns.reshape(pixels, -1), preferred_el...]
    unnamed x81 -> x60, local copies, waits for them, and re-layouts: 10.1 us -> 0.14 us
    ppermute x2 -> x0, local copies, waits for them, and re-layouts: 8.87 us -> none  [the longest x1 4.44 us: halo(): low = lax.ppermute(block[block.shape[0] - width:], axis, forward)]
    slice x2 -> x0, local copies, waits for them, and re-layouts: 7.29 us -> none  [the longest x1 5.3 us: halo(): low = lax.ppermute(block[block.shape[0] - width:], axis, forward)]
    ppermute x2 -> x0, starting transfers between devices: 6.88 us -> none  [the longest x1 5.46 us: halo(): high = lax.ppermute(block[:width], axis, backward)]
    concatenate x1 -> x0, other arithmetic: 6.15 us -> none  [halo(): return jnp.concatenate([low, block, high], axis=0)]
  transfers between devices with their start and end apart: 2 -> 0, of which waited for: 2 -> 0; matrix products, arithmetic and copies ran while one was open for 3% -> 0% of each run, Pallas kernels for 0% -> 0%
where the time goes in v2:
time: 349 us; the launch traced here: 344 us
  Pallas kernels  266 us (76%)
  matrix products  32.5 us (9%)
  local copies, waits for them, and re-layouts  25.9 us (7%)
  other arithmetic  17.8 us (5%)
    pallas_call x1, Pallas kernels, per_device(): pl.pallas_call(functools.partial(forward_kernel, n_rows, total_pixels), o...  145 us
    pallas_call x1, Pallas kernels, per_device(): pl.pallas_call(functools.partial(reduce_kernel, n_rows), out_shape=jax.Sh...  67.2 us
    pallas_call x1, Pallas kernels, per_device(): pl.pallas_call(gather_kernel, out_shape=(jax.ShapeDtypeStruct((4, own, 4...  53.6 us
    dot_general x10, matrix products, product(): jnp.einsum('pc,pd->cd', window, columns.reshape(pixels, -1), preferred_el...  26.9 us

profile of v2, /device:TPU:29, one launch (start us, length us, event | category | flops | bytes accessed | tf_op | source)
XLA Modules:
  0.0 344.4 jit_solution(17801332762549147822)
XLA Ops:
  0.7 2.4 convert_reduce_fusion
  3.1 0.8 compare_convert_fusion
  4.5 1.4 fusion.77
  5.9 1.5 fusion.76
  7.4 1.5 reshape.189.dw
  9.0 145.5 %shard_map.110 = (f32[768,1024]{1,0:T(8,128)}, bf16[60,128,512]{2,1,0:T(8,128)(2,1)}, bf16[4,5,64,256]{3,2,1,0:T(8,128)(2,1)}, f32[8,256]{1,0:T(8,128)}, f32[8,512]{1,0:T(8,128)}) custom-call(bf16[24,128,512]{2,1,0:T(8,128)(2,1)} %features.1, f32[27,512]{1,0:T(8,128)} %reshape.189.dw, bf16[4,512,256]{2,1,0:T(8,128)(2,1)} %weight.1, ...), custom_call_target="tpu_custom_call" | custom-call | tf_op jit(solution)/shard_map/pallas_call | solution.py:411
  154.5 0.7 convert_reduce_fusion.2
  155.3 1.0 fusion.49
  156.3 1.3 slice.364
  157.6 1.2 slice.368
  158.9 2.5 convolution_add_fusion
  162.2 0.7 maximum_maximum_fusion.small
  163.5 1.8 select_convert_fusion.grad
  165.3 1.1 copy.24
  166.3 53.6 %shard_map.111 = (bf16[4,768,1024]{2,1,0:T(8,128)(2,1)}, f32[256,256]{1,0:T(8,128)}, f32[16,256]{1,0:T(8,128)}) custom-call(bf16[768,1024]{1,0:T(8,128)(2,1)} %select_convert_fusion.grad, f32[4,256,256]{2,1,0:T(8,128)} %bitcast.144, f32[16,256]{1,0:T(8,128)} %maximum_maximum_fusion.small), custom_call_target="tpu_custom_call" | custom-call | tf_op jit(solution)/shard_map/pallas_call | solution.py:488
  220.0 0.9 convert.166
  220.9 1.1 convert.165
  222.0 2.4 fusion.18
  224.5 0.9 fusion.73
  225.3 1.0 fusion.74
  226.4 1.1 fusion.75
  228.1 2.7 convolution_bitcast_fusion.7
  230.8 2.9 convolution_bitcast_fusion.6
  233.8 2.7 convolution_bitcast_fusion.8
  236.6 1.6 add_convert_fusion.2
  238.2 2.7 convolution_bitcast_fusion.1
  240.9 2.7 convolution_bitcast_fusion
  243.6 0.8 fusion.48
  244.4 2.7 convolution_bitcast_fusion.2
  247.2 1.8 add_convert_fusion
  252.4 2.7 convolution_bitcast_fusion.4
  255.1 2.7 convolution_bitcast_fusion.3
  257.8 2.7 convolution_bitcast_fusion.5
  260.5 0.8 fusion.45
  261.3 0.8 fusion.42
  262.1 0.9 add_convert_fusion.1
  263.5 0.9 concatenate.23
  264.3 1.1 pad.34
  265.5 67.2 %shard_map.112 = f32[8,304,256]{2,1,0:T(8,128)} custom-call(bf16[8,304,256]{2,1,0:T(8,128)(2,1)} %bitcast.141), custom_call_target="tpu_custom_call" | custom-call | tf_op jit(solution)/shard_map/pallas_call | solution.py:545
  332.7 0.7 slice.409
  333.4 1.0 fusion.50
  334.5 0.8 maximum_convert_fusion.6
  335.3 1.3 slice_bitcast_fusion
  336.7 0.8 slice.408
  338.2 1.0 slice.410
  339.2 3.0 slice.407
  342.3 0.7 pad_maximum_fusion
  343.0 0.9 broadcast_multiply_fusion
  (104 shorter events, 7.5 us)
Async XLA Ops:
  0.6 160.7 %copy-start = (bf16[256,11]{0,1:T(8,128)(2,1)S(1)}, bf16[256,11]{0,1:T(8,128)(2,1)}, u32[]{:S(2)}) copy-start(bf16[256,11]{0,1:T(8,128)(2,1)} %param.12) | copy-start | bytes 16900
  157.6 5.3 %copy-start.2 = (f32[768,1024]{1,0:T(8,128)S(1)}, f32[768,1024]{1,0:T(8,128)}, u32[]{:S(2)}) copy-start(f32[768,1024]{1,0:T(8,128)} %get-tuple-element.14) | copy-start | bytes 9437188
  162.9 59.1 %slice-start = ((s8[7864320]{0:T(1024)(128)(4,1)}), s8[4194304]{0:T(1024)(128)(4,1)S(1)}, s32[]{:S(2)}) async-start(s8[7864320]{0:T(1024)(128)(4,1)} %bitcast.146), calls=%async_computation | async-start | bytes 8388608
  163.5 58.5 %slice-start.1 = ((s8[7864320]{0:T(1024)(128)(4,1)}), s8[3670016]{0:T(1024)(128)(4,1)S(1)}, s32[]{:S(2)}) async-start(s8[7864320]{0:T(1024)(128)(4,1)} %bitcast.146), calls=%async_computation.1 | async-start | bytes 7340032
  220.0 4.5 %copy-start.1 = (bf16[4,768,1024]{2,1,0:T(8,128)(2,1)S(1)}, bf16[4,768,1024]{2,1,0:T(8,128)(2,1)}, u32[]{:S(2)}) copy-start(bf16[4,768,1024]{2,1,0:T(8,128)(2,1)} %get-tuple-element.17) | copy-start | bytes 18874372
  233.7 2.8 copy-start.12
  233.7 2.8 copy-start.13
  233.7 2.8 copy-start.14
  233.7 2.8 copy-start.15
  233.8 2.8 copy-start.16
  233.8 2.8 copy-start.17
  233.8 2.8 copy-start.18
  233.8 2.8 copy-start.19
  233.8 2.8 copy-start.20
  240.9 2.7 copy-start.3
  244.4 2.8 copy-start.6
  244.4 2.8 copy-start.7
  244.4 2.8 copy-start.8
  244.4 2.8 copy-start.9
  244.4 2.8 copy-start.10
  244.4 2.8 copy-start.11
  261.2 2.0 copy-start.22
  261.2 2.0 copy-start.23
  261.2 2.0 copy-start.24
  261.2 2.0 copy-start.25
  261.3 2.0 copy-start.26
  261.3 2.0 copy-start.27
  261.3 2.2 copy-start.4
  261.3 2.2 copy-start.5
  265.4 77.6 %copy-start.21 = (f32[1,512]{1,0:T(1,128)S(1)}, f32[1,512]{1,0:T(1,128)}, u32[]{:S(2)}) copy-start(f32[1,512]{1,0:T(1,128)} %slice.364) | copy-start | bytes 6148

commit v3 on v2

--- a/solution.py
+++ b/solution.py
@@ -290,89 +290,206 @@
             down[t].wait_send()
 
 
-def gather_kernel(
-    grad, proj, small, grad_out, proj_out, small_out, slots, proj_slots, small_slots,
-    big_send, big_recv, proj_send, proj_recv, small_send, small_recv,
+def backward_kernel(
+    n_rows,
+    grad,
+    proj,
+    small,
+    f,
+    dw,
+    weight_t,
+    branch_out,
+    rest_out,
+    grads,
+    acc,
+    depth,
+    terms,
+    rest,
+    landed,
+    landed_rest,
+    total,
+    total_rest,
+    gathered,
+    gathered_rest,
+    proj_slots,
+    small_slots,
+    big_send,
+    big_recv,
+    proj_send,
+    proj_recv,
+    small_send,
+    small_recv,
+    s_send,
+    s_recv,
+    g_send,
+    g_recv,
 ):
     me_r, me_g = lax.axis_index("rows"), lax.axis_index("grp")
-    grp_peers = [(me_r, lax.rem(me_g + j, 4)) for j in range(1, 4)]
-    greet(grp_peers)
+    row_peers, grp_peers = places_of(n_rows, 4, me_r, me_g)
+    greet(row_peers + grp_peers)
     mate = me_g + 1 - 2 * lax.rem(me_g, 2)
     x_peer = lax.rem(me_g + 2, 4)
-    diag = lax.rem(mate + 2, 4)
-    pieces = 4
-    step = grad.shape[0] // pieces
-    spans = [slice(p * step, (p + 1) * step) for p in range(pieces)]
-    crossing = []
-    for p, span in enumerate(spans):
-        copy = remote(
-            grad.at[span], slots.at[1, span], big_send.at[1 + p], big_recv.at[1 + p], me_r, x_peer
-        )
-        copy.start()
-        crossing.append(copy)
-    near = remote(grad, slots.at[0], big_send.at[0], big_recv.at[0], me_r, mate)
-    near.start()
+    height = f.shape[0] - 2 * MARGIN
+    width, channels = f.shape[1], f.shape[2]
+    hold = grad.shape[1]
+    own = grad.shape[2]
+    halves = channels // 256
+
+    crossing, near = [], []
+    for k in range(4):
+        one = remote(
+            grad.at[k], grads.at[me_g, k], big_send.at[k], big_recv.at[k], me_r, x_peer
+        )
+        two = remote(
+            grad.at[k], grads.at[me_g, k], big_send.at[4 + k], big_recv.at[4 + k], me_r, mate
+        )
+        one.start()
+        two.start()
+        crossing.append(one)
+        near.append(two)
     others = []
     for j, (pr, pg) in enumerate(grp_peers):
-        one = remote(proj.at[pg], proj_slots.at[j], proj_send.at[j], proj_recv.at[j], pr, pg)
+        one = remote(proj.at[pg], proj_slots.at[me_g], proj_send.at[j], proj_recv.at[j], pr, pg)
         two = remote(small, small_slots.at[me_g], small_send.at[j], small_recv.at[j], pr, pg)
         one.start()
         two.start()
         others += [one, two]
+    proj_slots[me_g] = proj[me_g]
     small_slots[me_g] = small[...]
-    grad_out[me_g] = grad[...]
-    near.wait()
-    grad_out[mate] = slots[0]
+    grads[me_g] = grad[...]
+    depth[...] = jnp.zeros(depth.shape, F32)
+    lane = lax.broadcasted_iota(jnp.int32, (hold, width), 1)
+    pairs = own // (2 * width)
+
+    def products(k):
+        acc[...] = jnp.zeros(acc.shape, F32)
+
+        def step(p, carry):
+            q, within = p // pairs, lax.rem(p, pairs)
+            at = pl.ds(pl.multiple_of(within * 2 * width, 2 * width), 2 * width)
+            block = grads[q, k, :, at]
+            if k == 0:
+                rows = f[pl.ds(p * 2 + MARGIN, 2)].reshape(2 * width, channels)
+                acc[0, :hold] += jnp.dot(block, rows, preferred_element_type=F32)
+                return carry
+            rate = RATES[k - 1]
+            wide = block.astype(F32)
+            lefts, rights = [], []
+            for i in range(2):
+                x = wide[:, i * width : (i + 1) * width]
+                lefts.append(
+                    jnp.where(lane < width - rate, pltpu.roll(x, width - rate, 1), 0.0)
+                )
+                rights.append(jnp.where(lane >= rate, pltpu.roll(x, rate, 1), 0.0))
+            left = jnp.concatenate(lefts, axis=1).astype(BF16)
+            right = jnp.concatenate(rights, axis=1).astype(BF16)
+            for a in range(3):
+                rows = f[pl.ds(p * 2 + MARGIN + (a - 1) * rate, 2)].reshape(2 * width, channels)
+                for b, lhs in enumerate((left, block, right)):
+                    acc[a, b * hold : (b + 1) * hold] += jnp.dot(
+                        lhs, rows, preferred_element_type=F32
+                    )
+            return carry
+
+        lax.fori_loop(0, height // 2, step, 0)
+
+    def spread(unit, source, target):
+        copies = []
+        for j, (pr, pg) in enumerate(row_peers):
+            at = unit * (n_rows - 1) + j
+            copy = remote(source(pr), target, s_send.at[at], s_recv.at[at], pr, pg)
+            copy.start()
+            copies.append(copy)
+        return copies
+
+    def share(unit, source, target):
+        copies = []
+        for j, (pr, pg) in enumerate(row_peers):
+            at = unit * (n_rows - 1) + j
+            copy = remote(source, target, g_send.at[at], g_recv.at[at], pr, pg)
+            copy.start()
+            copies.append(copy)
+        return copies
+
+    def add_up(parts):
+        value = parts[0].astype(F32)
+        for j in range(1, n_rows):
+            value = value + parts[j].astype(F32)
+        return value.astype(BF16)
+
+    spreading, sharing = [], []
+
+    def finish(k):
+        for copy in spreading[k]:
+            copy.wait()
+        total[k] = add_up([landed[k, j] for j in range(n_rows)])
+        gathered[k, me_r] = total[k]
+        sharing.append(share(k, total.at[k], gathered.at[k, me_r]))
+
+    span = terms.shape[2]
     passing = []
-    for p, span in enumerate(spans):
-        crossing[p].wait()
+    for k in range(4):
+        crossing[k].wait()
         copy = remote(
-            slots.at[1, span],
-            slots.at[2, span],
-            big_send.at[1 + pieces + p],
-            big_recv.at[1 + pieces + p],
+            grads.at[x_peer, k],
+            grads.at[x_peer, k],
+            big_send.at[8 + k],
+            big_recv.at[8 + k],
             me_r,
             mate,
         )
         copy.start()
         passing.append(copy)
-    grad_out[x_peer] = slots[1]
+        near[k].wait()
+        copy.wait()
+        products(k)
+        if k == 0:
+            value = acc[0, :hold]
+        else:
+            value = jnp.zeros((hold, channels), F32)
+            for a in range(3):
+                for b in range(3):
+                    at = (k - 1) * 9 + a * 3 + b
+                    term = acc[a, b * hold : (b + 1) * hold]
+                    value = value + dw[at : at + 1, :] * term
+                    depth[at : at + 1, :] = jnp.sum(
+                        weight_t[k - 1].astype(F32) * term, axis=0, keepdims=True
+                    )
+        flat = jnp.concatenate(
+            [value[:, c * 256 : (c + 1) * 256] for c in range(halves)], axis=0
+        ).astype(BF16)
+        terms[k] = flat.reshape(n_rows, span, 256)
+        landed[k, me_r] = terms[k, me_r]
+        spreading.append(
+            spread(k, lambda pr, k=k: terms.at[k, pr], landed.at[k, me_r])
+        )
+        if k > 0:
+            finish(k - 1)
+
     for copy in others:
         copy.wait()
-    proj_out[...] = (
-        proj[me_g] + proj_slots[0] + proj_slots[1] + proj_slots[2]
-    )
-    small_out[...] = small_slots[0] + small_slots[1] + small_slots[2] + small_slots[3]
-    for copy in passing:
+    lines = [depth[:, c * 256 : (c + 1) * 256] for c in range(halves)]
+    lines.append(proj_slots[0] + proj_slots[1] + proj_slots[2] + proj_slots[3])
+    lines.append(small_slots[0] + small_slots[1] + small_slots[2] + small_slots[3])
+    flat = jnp.concatenate(lines, axis=0)
+    spare = rest.shape[0] * rest.shape[1] - flat.shape[0]
+    flat = jnp.concatenate([flat, jnp.zeros((spare, 256), F32)], axis=0).astype(BF16)
+    rest[...] = flat.reshape(rest.shape)
+    landed_rest[me_r] = rest[me_r]
+    last = spread(4, lambda pr: rest.at[pr], landed_rest.at[me_r])
+    finish(3)
+    for copy in last:
         copy.wait()
-    grad_out[diag] = slots[2]
-
-
-def reduce_kernel(n_rows, terms, out, landed, total, gathered, s_send, s_recv, g_send, g_recv):
-    me_r, me_g = lax.axis_index("rows"), lax.axis_index("grp")
-    row_peers = [(lax.rem(me_r + j, n_rows), me_g) for j in range(1, n_rows)]
-    greet(row_peers)
-    copies = []
-    for j, (pr, pg) in enumerate(row_peers):
-        copy = remote(terms.at[pr], landed.at[me_r], s_send.at[j], s_recv.at[j], pr, pg)
-        copy.start()
-        copies.append(copy)
-    landed[me_r] = terms[me_r]
-    for copy in copies:
+    total_rest[...] = add_up([landed_rest[j] for j in range(n_rows)])
+    gathered_rest[me_r] = total_rest[...]
+    last = share(4, total_rest, gathered_rest.at[me_r])
+    for k in range(4):
+        for copy in sharing[k]:
+            copy.wait()
+        branch_out[k] = gathered[k].astype(F32)
+    for copy in last:
         copy.wait()
-    value = landed[0].astype(F32)
-    for j in range(1, n_rows):
-        value = value + landed[j].astype(F32)
-    total[...] = value.astype(BF16)
-    copies = []
-    for j, (pr, pg) in enumerate(row_peers):
-        copy = remote(total, gathered.at[me_r], g_send.at[j], g_recv.at[j], pr, pg)
-        copy.start()
-        copies.append(copy)
-    gathered[me_r] = total[...]
-    for copy in copies:
-        copy.wait()
-    out[...] = gathered[...].astype(F32)
+    rest_out[...] = gathered_rest[...].astype(F32)
 
 
 def params(number):
@@ -383,15 +500,6 @@
 
 def dma(count):
     return pltpu.SemaphoreType.DMA((count,))
-
-
-def slide(block, shift):
-    if shift == 0:
-        return block
-    width = block.shape[1]
-    if shift > 0:
-        return jnp.pad(block[:, : width - shift], ((0, 0), (shift, 0), (0, 0)))
-    return jnp.pad(block[:, -shift:], ((0, 0), (0, -shift), (0, 0)))
 
 
 def per_device(
@@ -484,90 +592,69 @@
         [class_part, col_part[None], jnp.zeros((small_rows - classes - 1, hold), F32)], axis=0
     )
 
-    pieces = 4
-    grad_all, proj_sum, small_sum = pl.pallas_call(
-        gather_kernel,
+    halves = channels // 256
+    depth_lines = 32
+    span = halves * hold // n_rows
+    rest_used = halves * depth_lines + hold + small_rows
+    rest_span = -(-rest_used // (n_rows * 16)) * 16
+    branch_full, rest_full = pl.pallas_call(
+        functools.partial(backward_kernel, n_rows),
         out_shape=(
-            jax.ShapeDtypeStruct((4, own, 4 * hold), BF16),
-            jax.ShapeDtypeStruct((hold, hold), F32),
-            jax.ShapeDtypeStruct((small_rows, hold), F32),
+            jax.ShapeDtypeStruct((4, n_rows, span, 256), F32),
+            jax.ShapeDtypeStruct((n_rows, rest_span, 256), F32),
         ),
-        in_specs=[vspec()] * 3,
-        out_specs=(vspec(),) * 3,
+        in_specs=[vspec()] * 6,
+        out_specs=(vspec(),) * 2,
         scratch_shapes=[
-            pltpu.VMEM((3, own, 4 * hold), BF16),
-            pltpu.VMEM((3, hold, hold), F32),
+            pltpu.VMEM((4, 4, hold, own), BF16),
+            pltpu.VMEM((3, 3 * hold, channels), F32),
+            pltpu.VMEM((depth_lines, channels), F32),
+            pltpu.VMEM((4, n_rows, span, 256), BF16),
+            pltpu.VMEM((n_rows, rest_span, 256), BF16),
+            pltpu.VMEM((4, n_rows, span, 256), BF16),
+            pltpu.VMEM((n_rows, rest_span, 256), BF16),
+            pltpu.VMEM((4, span, 256), BF16),
+            pltpu.VMEM((rest_span, 256), BF16),
+            pltpu.VMEM((4, n_rows, span, 256), BF16),
+            pltpu.VMEM((n_rows, rest_span, 256), BF16),
+            pltpu.VMEM((4, hold, hold), F32),
             pltpu.VMEM((4, small_rows, hold), F32),
-            dma(1 + 2 * pieces),
-            dma(1 + 2 * pieces),
-            dma(3),
-            dma(3),
-            dma(3),
-            dma(3),
+            dma(12),
+            dma(12),
+            dma(3),
+            dma(3),
+            dma(3),
+            dma(3),
+            dma(5 * (n_rows - 1)),
+            dma(5 * (n_rows - 1)),
+            dma(5 * (n_rows - 1)),
+            dma(5 * (n_rows - 1)),
         ],
         compiler_params=params(1),
-    )(grad_pre, proj_part, small)
-
-    grad_all = grad_all.reshape(height, width, 4 * hold)
-    pixels = height * width
-
-    def product(shift, columns):
-        window = padded[MARGIN + shift : MARGIN + shift + height].reshape(pixels, channels)
-        return jnp.einsum(
-            "pc,pd->cd", window, columns.reshape(pixels, -1), preferred_element_type=F32
-        )
-
-    slid = []
-    for r, rate in enumerate(RATES):
-        part = grad_all[:, :, (r + 1) * hold : (r + 2) * hold]
-        slid.append(
-            jnp.concatenate([slide(part, (b - 1) * rate) for b in range(3)], axis=2)
-        )
-    branch_rows = [product(0, grad_all[:, :, :hold])]
-    depth_rows = []
-    for r, rate in enumerate(RATES):
-        branch_sum = jnp.zeros((channels, hold), F32)
-        for a in range(3):
-            g = product((a - 1) * rate, slid[r])
-            for b in range(3):
-                term = g[:, b * hold : (b + 1) * hold]
-                branch_sum = branch_sum + depth_weight[r, a, b][:, None] * term
-                depth_rows.append(jnp.sum(term * branch_weight[r + 1].astype(F32), axis=1))
-        branch_rows.append(branch_sum)
-    depth_part = jnp.stack(depth_rows)
-
-    terms = jnp.concatenate(
-        branch_rows + [depth_part.reshape(-1, hold), proj_sum, small_sum], axis=0
-    ).astype(BF16)
-    used = terms.shape[0]
-    span = -(-used // (n_rows * 16)) * 16
-    terms = jnp.pad(terms, ((0, span * n_rows - used), (0, 0))).reshape(n_rows, span, hold)
-    full = pl.pallas_call(
-        functools.partial(reduce_kernel, n_rows),
-        out_shape=jax.ShapeDtypeStruct((n_rows, span, hold), F32),
-        in_specs=[vspec()],
-        out_specs=vspec(),
-        scratch_shapes=[
-            pltpu.VMEM((n_rows, span, hold), BF16),
-            pltpu.VMEM((span, hold), BF16),
-            pltpu.VMEM((n_rows, span, hold), BF16),
-            dma(n_rows - 1),
-            dma(n_rows - 1),
-            dma(n_rows - 1),
-            dma(n_rows - 1),
-        ],
-        compiler_params=params(2),
-    )(terms)
-    full = full.reshape(n_rows * span, hold)
-    at = 4 * channels
-    grad_branch = full[:at].reshape(4, channels, hold)
-    depth_len = 27 * channels // hold
-    grad_depth = full[at : at + depth_len].reshape(3, 3, 3, channels)
-    at += depth_len
-    proj_main_grad = full[at : at + hold].reshape(4, own_hold, hold)
+    )(
+        grad_pre.T.reshape(4, hold, own),
+        proj_part,
+        small,
+        padded,
+        dw,
+        branch_weight[1:].transpose(0, 2, 1),
+    )
+    grad_branch = (
+        branch_full.reshape(4, halves, hold, 256).transpose(0, 1, 3, 2).reshape(4, channels, hold)
+    )
+    rest = rest_full.reshape(n_rows * rest_span, 256)
+    at = halves * depth_lines
+    grad_depth = (
+        rest[:at]
+        .reshape(halves, depth_lines, 256)
+        .transpose(1, 0, 2)
+        .reshape(depth_lines, channels)[:27]
+        .reshape(3, 3, 3, channels)
+    )
+    proj_main_grad = rest[at : at + hold].reshape(4, own_hold, hold)
     at += hold
-    grad_class = full[at : at + classes].T
-    col_total = full[at + classes]
+    grad_class = rest[at : at + classes].T
+    col_total = rest[at + classes]
     back_pool = jnp.sum(proj_all[4].astype(F32) * col_total[None, :], axis=1)
     grad_poolpre = (back_pool * (pool_pre > 0)).astype(BF16)
     grad_pool = pooled[:, None] * grad_poolpre.astype(F32)[None, :]

time: 349 us -> 282 us (0.81)
  matrix products: 32.5 us -> 8.17 us
  Pallas kernels: 266 us -> 243 us
  other arithmetic: 17.8 us -> 9.19 us
  local copies, waits for them, and re-layouts: 25.9 us -> 17.5 us
    dot_general x10 -> x0, matrix products: 26.9 us -> none  [product(): jnp.einsum('pc,pd->cd', window, columns.reshape(pixels, -1), preferred_el...]
    pallas_call x2 -> x1, Pallas kernels: 121 us -> 97.7 us  [per_device(): pl.pallas_call(functools.partial(backward_kernel, n_rows), out_shape=(jax...]
    slice x10 -> x6, local copies, waits for them, and re-layouts: 12.1 us -> 2.58 us  [the longest x1 0.97 us: per_device(): proj_main_grad = rest[at:at + hold].reshape(4, own_hold, hold)]
    another operation x5 -> x0, other arithmetic: 6.3 us -> none
    transpose x1 -> x3, local copies, waits for them, and re-layouts: 1.34 us -> 6.86 us  [the longest x1 2.88 us: per_device(): branch_full.reshape(4, halves, hold, 256).transpose(0, 1, 3, 2)]
    another operation x28 -> x0, local copies, waits for them, and re-layouts: 3.6 us -> none  [per_device(): depth_part = jnp.stack(depth_rows)]
where the time goes in v3:
time: 282 us; the launch traced here: 279 us
  Pallas kernels  243 us (86%)
  local copies, waits for them, and re-layouts  17.5 us (6%)
  other arithmetic  9.19 us (3%)
  matrix products  8.17 us (3%)
    pallas_call x1, Pallas kernels, per_device(): pl.pallas_call(functools.partial(forward_kernel, n_rows, total_pixels), o...  145 us
    pallas_call x1, Pallas kernels, per_device(): pl.pallas_call(functools.partial(backward_kernel, n_rows), out_shape=(jax...  97.7 us

profile of v3, /device:TPU:29, one launch (start us, length us, event | category | flops | bytes accessed | tf_op | source)
XLA Modules:
  0.0 278.8 jit_solution(1937477109191913996)
XLA Ops:
  0.6 0.0 copy-start
  0.6 1.5 reshape.138.dw
  2.2 2.4 convert_reduce_fusion
  4.6 0.6 broadcast_in_dim.6.col_sum
  5.2 145.4 %shard_map.110 = (f32[768,1024]{1,0:T(8,128)}, bf16[60,128,512]{2,1,0:T(8,128)(2,1)}, bf16[4,5,64,256]{3,2,1,0:T(8,128)(2,1)}, f32[8,256]{1,0:T(8,128)}, f32[8,512]{1,0:T(8,128)}) custom-call(bf16[24,128,512]{2,1,0:T(8,128)(2,1)} %features.1, f32[27,512]{1,0:T(8,128)} %reshape.138.dw, bf16[4,512,256]{2,1,0:T(8,128)(2,1)} %weight.1, ...), custom_call_target="tpu_custom_call" | custom-call | tf_op jit(solution)/shard_map/pallas_call | solution.py:519
  150.6 0.7 convert_reduce_fusion.2
  151.3 0.1 reshape.150
  151.4 1.0 fusion.3
  152.4 1.1 slice.44
  153.6 0.0 copy-start.3
  153.6 0.0 copy-start.1
  153.6 2.7 convolution_add_fusion
  156.3 0.0 copy-start.2
  156.3 0.9 copy-done.2
  157.2 0.0 copy-done
  157.2 0.3 fusion.17
  157.5 0.0 copy-done.3
  157.5 0.8 compare_convert_fusion
  158.3 1.3 fusion.5
  159.6 1.5 convert_reduce_fusion.1
  161.1 0.1 pad.4.clone
  161.2 0.7 maximum_maximum_fusion.small
  161.8 0.0 copy-done.1
  161.9 0.0 copy-start.4
  161.9 0.6 fusion.2
  162.5 1.1 copy.19
  163.6 0.0 copy-done.4
  163.6 1.8 fusion
  165.3 0.0 slice-start
  165.3 2.7 copy.18
  168.0 0.0 slice-done
  168.0 1.2 copy.23
  169.1 97.7 %shard_map.111 = (f32[4,8,64,256]{3,2,1,0:T(8,128)}, f32[8,48,256]{2,1,0:T(8,128)}) custom-call(bf16[4,256,768]{2,1,0:T(8,128)(2,1)} %bitcast.48, f32[4,256,256]{2,1,0:T(8,128)} %bitcast.52, f32[16,256]{1,0:T(8,128)} %maximum_maximum_fusion.small, bf16[60,128,512]{2,1,0:T(8,128)(2,1)} %get-tuple-element.15.f, f32[27,512]{1,0:T(8,128)} %reshape.138.dw, ...), custom_call_target="tpu_custom_call" | custom-call | tf_op jit(solution)/shard_map/pallas_call | solution.py:600
  266.9 0.7 slice.48
  267.6 1.0 fusion.4
  268.6 0.1 reduce_sum.52
  268.7 0.8 maximum_convert_fusion.6
  269.5 0.1 bitcast_convert_fusion
  269.6 0.1 broadcast_multiply_fusion.1
  269.7 1.0 slice.49
  270.6 0.7 pad_maximum_fusion
  271.4 0.7 slice.40
  272.1 0.9 broadcast_multiply_fusion
  273.0 2.9 %copy.21 = f32[4,2,256,256]{3,2,1,0:T(8,128)} copy(f32[4,2,256,256]{2,3,1,0:T(8,128)} %bitcast.54) | data formatting | bytes 4194304 | tf_op jit(solution)/shard_map/transpose | solution.py:643
  275.9 0.8 slice.46
  276.8 0.7 reshape.148
  277.5 1.3 slice_bitcast_fusion
  (3 shorter events, 0.1 us)
Async XLA Ops:
  0.6 156.6 %copy-start = (bf16[256,11]{0,1:T(8,128)(2,1)S(1)}, bf16[256,11]{0,1:T(8,128)(2,1)}, u32[]{:S(2)}) copy-start(bf16[256,11]{0,1:T(8,128)(2,1)} %param.12) | copy-start | bytes 16900
  153.6 3.9 %copy-start.3 = (bf16[4,4,64,256]{3,2,1,0:T(8,128)(2,1)}, bf16[4,4,64,256]{3,2,1,0:T(8,128)(2,1)S(1)}, u32[]{:S(2)}) copy-start(bf16[4,4,64,256]{3,2,1,0:T(8,128)(2,1)S(1)} %copy.17) | copy-start | bytes 1572868
  153.6 8.3 %copy-start.1 = (f32[768,1024]{1,0:T(8,128)S(1)}, f32[768,1024]{1,0:T(8,128)}, u32[]{:S(2)}) copy-start(f32[768,1024]{1,0:T(8,128)} %get-tuple-element.12) | copy-start | bytes 9437188
  156.3 0.9 copy-start.2
  161.9 1.7 copy-start.4
  165.3 2.7 slice-start

commit v4 on v3

--- a/solution.py
+++ b/solution.py
@@ -50,7 +50,6 @@
     features,
     dw,
     weight,
-    col_sum,
     pool_weight,
     proj,
     pre_out,
@@ -64,6 +63,7 @@
     from_mate,
     to_x,
     from_x,
+    col_sum,
     sums,
     parts,
     projs,
@@ -137,12 +137,6 @@
     def _():
         f[pl.ds(MARGIN + height, MARGIN)] = jnp.zeros((MARGIN, width, channels), BF16)
 
-    sums[me_r] = col_sum[...]
-    sum_copies = []
-    for j, (pr, pg) in enumerate(row_peers):
-        copy = remote(col_sum, sums.at[me_r], sum_send.at[j], sum_recv.at[j], pr, pg)
-        copy.start()
-        sum_copies.append(copy)
     projs[me_g] = proj[...]
     proj_copies = []
     for j, (pr, pg) in enumerate(grp_peers):
@@ -167,11 +161,9 @@
                         taps = [f[h + (a - 1) * rate, :, ch].astype(F32) for a in range(3)]
                         sides = []
                         for b in range(3):
-                            at = (k - 1) * 9 + b
+                            gains = [dw[k - 1, a, b : b + 1, ch] for a in range(3)]
                             sides.append(
-                                dw[at : at + 1, ch] * taps[0]
-                                + dw[at + 3 : at + 4, ch] * taps[1]
-                                + dw[at + 6 : at + 7, ch] * taps[2]
+                                gains[0] * taps[0] + gains[1] * taps[1] + gains[2] * taps[2]
                             )
                         left = jnp.where(column >= rate, pltpu.roll(sides[0], rate, 0), 0.0)
                         right = jnp.where(
@@ -232,6 +224,19 @@
         quarter(me_g, k, put_own)
 
     middle.wait()
+
+    def add_row(h, held):
+        row = f[MARGIN + h].astype(F32)
+        return held + jnp.sum(row.reshape(width // 8, 8, channels), axis=0)
+
+    held = lax.fori_loop(0, height, add_row, jnp.zeros((8, channels), F32))
+    col_sum[...] = jnp.broadcast_to(jnp.sum(held, axis=0, keepdims=True), (8, channels))
+    sums[me_r] = col_sum[...]
+    sum_copies = []
+    for j, (pr, pg) in enumerate(row_peers):
+        copy = remote(col_sum, sums.at[me_r], sum_send.at[j], sum_recv.at[j], pr, pg)
+        copy.start()
+        sum_copies.append(copy)
     branch(0)
     for copy in sum_copies:
         copy.wait()
@@ -451,7 +456,7 @@
                 for b in range(3):
                     at = (k - 1) * 9 + a * 3 + b
                     term = acc[a, b * hold : (b + 1) * hold]
-                    value = value + dw[at : at + 1, :] * term
+                    value = value + dw[k - 1, a, b : b + 1, :] * term
                     depth[at : at + 1, :] = jnp.sum(
                         weight_t[k - 1].astype(F32) * term, axis=0, keepdims=True
                     )
@@ -513,8 +518,7 @@
     classes = class_weight.shape[1]
     total_pixels = height * n_rows * width
     own = height * width // 4
-    col_sum = jnp.sum(features.astype(F32), axis=(0, 1))
-    dw = depth_weight.reshape(27, channels)
+    dw = depth_weight
 
     pre, padded, projs, pool_pre8, pooled8 = pl.pallas_call(
         functools.partial(forward_kernel, n_rows, total_pixels),
@@ -525,7 +529,7 @@
             jax.ShapeDtypeStruct((8, hold), F32),
             jax.ShapeDtypeStruct((8, channels), F32),
         ),
-        in_specs=[pl.BlockSpec(memory_space=pl.ANY)] + [vspec()] * 5,
+        in_specs=[pl.BlockSpec(memory_space=pl.ANY)] + [vspec()] * 4,
         out_specs=(vspec(),) * 5,
         scratch_shapes=[
             pltpu.VMEM((2 * width, channels), BF16),
@@ -534,6 +538,7 @@
             pltpu.VMEM((4, 2, own, hold), BF16),
             pltpu.VMEM((4, own, hold), BF16),
             pltpu.VMEM((4, own, hold), BF16),
+            pltpu.VMEM((8, channels), F32),
             pltpu.VMEM((n_rows, 8, channels), F32),
             pltpu.VMEM((4, 8, hold), F32),
             pltpu.VMEM((4,) + proj_weight.shape, BF16),
@@ -556,7 +561,6 @@
         features,
         dw,
         branch_weight,
-        jnp.broadcast_to(col_sum[None], (8, channels)),
         pool_weight,
         proj_weight,
     )

time: 282 us -> 278 us (0.986)
  no operation moved by 1% of the time
where the time goes in v4:
time: 278 us; the launch traced here: 274 us
  Pallas kernels  243 us (87%)
  local copies, waits for them, and re-layouts  15.3 us (6%)
  matrix products  8.17 us (3%)
  other arithmetic  6.82 us (2%)
    pallas_call x1, Pallas kernels, per_device(): pl.pallas_call(functools.partial(forward_kernel, n_rows, total_pixels), o...  145 us
    pallas_call x1, Pallas kernels, per_device(): pl.pallas_call(functools.partial(backward_kernel, n_rows), out_shape=(jax...  97.7 us

profile of v4, /device:TPU:29, one launch (start us, length us, event | category | flops | bytes accessed | tf_op | source)
XLA Modules:
  0.0 274.3 jit_solution(416532665077396337)
XLA Ops:
  0.6 0.0 copy-start
  0.6 145.4 %shard_map.110 = (f32[768,1024]{1,0:T(8,128)}, bf16[60,128,512]{2,1,0:T(8,128)(2,1)}, bf16[4,5,64,256]{3,2,1,0:T(8,128)(2,1)}, f32[8,256]{1,0:T(8,128)}, f32[8,512]{1,0:T(8,128)}) custom-call(bf16[24,128,512]{2,1,0:T(8,128)(2,1)} %features.1, f32[3,3,3,512]{3,2,1,0:T(4,128)} %dw.3, bf16[4,512,256]{2,1,0:T(8,128)(2,1)} %weight.1, ...), custom_call_target="tpu_custom_call" | custom-call | tf_op jit(solution)/shard_map/pallas_call | solution.py:523
  146.1 0.7 convert_reduce_fusion.1
  146.8 0.1 reshape.145
  146.9 1.0 fusion.3
  147.9 1.1 slice.44
  149.0 0.0 copy-start.3
  149.1 0.0 copy-start.1
  149.1 2.7 convolution_add_fusion
  151.8 0.0 copy-start.2
  151.8 0.9 copy-done.2
  152.7 0.0 copy-done
  152.7 0.3 fusion.17
  152.9 0.0 copy-done.3
  152.9 0.8 compare_convert_fusion
  153.7 1.3 fusion.5
  155.0 1.5 convert_reduce_fusion
  156.6 0.1 pad.4.clone
  156.6 0.7 maximum_maximum_fusion.small
  157.3 0.0 copy-done.1
  157.3 0.0 copy-start.4
  157.3 0.6 fusion.2
  157.9 1.1 copy.19
  159.0 0.0 copy-done.4
  159.0 1.8 fusion
  160.8 0.0 slice-start
  160.8 2.7 copy.18
  163.4 0.0 slice-done
  163.4 1.2 copy.23
  164.6 97.7 %shard_map.111 = (f32[4,8,64,256]{3,2,1,0:T(8,128)}, f32[8,48,256]{2,1,0:T(8,128)}) custom-call(bf16[4,256,768]{2,1,0:T(8,128)(2,1)} %bitcast.48, f32[4,256,256]{2,1,0:T(8,128)} %bitcast.51, f32[16,256]{1,0:T(8,128)} %maximum_maximum_fusion.small, bf16[60,128,512]{2,1,0:T(8,128)(2,1)} %get-tuple-element.15.f, f32[3,3,3,512]{3,2,1,0:T(4,128)} %dw.3, ...), custom_call_target="tpu_custom_call" | custom-call | tf_op jit(solution)/shard_map/pallas_call | solution.py:604
  262.4 0.7 slice.48
  263.1 1.0 fusion.4
  264.1 0.1 reduce_sum.42
  264.2 0.8 maximum_convert_fusion.6
  265.0 0.1 bitcast_convert_fusion
  265.0 0.1 broadcast_multiply_fusion.1
  265.1 1.0 slice.49
  266.1 0.7 pad_maximum_fusion
  266.8 0.7 slice.40
  267.6 0.9 broadcast_multiply_fusion
  268.5 2.9 %copy.21 = f32[4,2,256,256]{3,2,1,0:T(8,128)} copy(f32[4,2,256,256]{2,3,1,0:T(8,128)} %bitcast.54) | data formatting | bytes 4194304 | tf_op jit(solution)/shard_map/transpose | solution.py:647
  271.4 0.8 slice.46
  272.3 0.7 reshape.143
  272.9 1.3 slice_bitcast_fusion
  (3 shorter events, 0.1 us)
Async XLA Ops:
  0.6 152.0 %copy-start = (bf16[256,11]{0,1:T(8,128)(2,1)S(1)}, bf16[256,11]{0,1:T(8,128)(2,1)}, u32[]{:S(2)}) copy-start(bf16[256,11]{0,1:T(8,128)(2,1)} %param.12) | copy-start | bytes 16900
  149.0 3.9 %copy-start.3 = (bf16[4,4,64,256]{3,2,1,0:T(8,128)(2,1)}, bf16[4,4,64,256]{3,2,1,0:T(8,128)(2,1)S(1)}, u32[]{:S(2)}) copy-start(bf16[4,4,64,256]{3,2,1,0:T(8,128)(2,1)S(1)} %copy.17) | copy-start | bytes 1572868
  149.1 8.3 %copy-start.1 = (f32[768,1024]{1,0:T(8,128)S(1)}, f32[768,1024]{1,0:T(8,128)}, u32[]{:S(2)}) copy-start(f32[768,1024]{1,0:T(8,128)} %get-tuple-element.12) | copy-start | bytes 9437188
  151.8 0.9 copy-start.2
  157.3 1.7 copy-start.4
  160.8 2.7 slice-start
